TPU v7x, 256 devices: a whole 4x4x8 slice. The times are simulated.
256 devices in a mesh: lat: 16 (over z_hi, y), lon: 2 (over z_lo), dp: 8 (over x, core).
Axes of the slice: x: 4, y: 4, z: 8 (z_hi: 4, z_lo: 2; z = z_hi * 2 + z_lo), core: 2. Of those that a mesh axis runs over, the one named last changes fastest.
Arguments:
- inputs: bfloat16 [8, 384, 128, 768], P('dp', 'lat', 'lon'), may hold values from -6 to 6
- cotangent: bfloat16 [8, 384, 128, 768], P('dp', 'lat', 'lon'), may hold values from -6 to 6
- weight: bfloat16 [384, 2, 128, 128], P(('lat', 'dp'), None, 'lon'), may hold values from -0.375 to 0.375
Outputs:
- input_grad: bfloat16 [8, 384, 128, 768], P('dp', 'lat', 'lon')
- weight_grad: float32 [384, 2, 128, 128], P(('lat', 'dp'), None, 'lon')
All inputs are finite; a program needn't handle non-finite values.
Results may differ from a plain program's by a relative error of at most 0.013.
Values may be sent and summed in bfloat16 or wider, within the bound.
A program may use at most 128 MiB of HBM per device.

v0:
```python
import math

import jax
import jax.numpy as jnp
from jax import lax
from jax.sharding import PartitionSpec as P

L = 384


def legendre_table(orders, lat_count, degrees):
    lat_index = jnp.arange(lat_count, dtype=jnp.float32)
    colatitude = math.pi * (lat_index + 0.5) / lat_count
    cosine = jnp.cos(colatitude)[None, :]
    sine_v = jnp.sin(colatitude)[None, :]
    step_nums = jnp.arange(1, degrees, dtype=jnp.float32)
    cumlog = jnp.concatenate(
        [jnp.zeros((1,), jnp.float32), jnp.cumsum(jnp.log1p(-0.5 / step_nums))]
    )
    selector = (orders[:, None] == jnp.arange(degrees, dtype=jnp.int32)[None, :]).astype(
        jnp.float32
    )
    order_log = jnp.sum(selector * cumlog[None, :], axis=1)
    order_f = orders.astype(jnp.float32)[:, None]
    log_start = 0.5 * (
        jnp.log(2.0 * order_f + 1.0) - math.log(4.0 * math.pi) + order_log[:, None]
    ) + order_f * jnp.log(sine_v)
    shift_up = jnp.clip(-log_start - 60.0, 0.0, 80.0)
    seed_row = jnp.exp(log_start + shift_up)
    unscale = jnp.exp(-shift_up)

    def advance(state_pair, degree):
        previous, before_prev = state_pair
        degree_f = degree.astype(jnp.float32)
        upward = jnp.sqrt(
            jnp.maximum(4.0 * degree_f * degree_f - 1.0, 1.0)
            / jnp.maximum(degree_f * degree_f - order_f * order_f, 1.0)
        )
        lower_deg = degree_f - 1.0
        backward = jnp.sqrt(
            jnp.maximum(lower_deg * lower_deg - order_f * order_f, 0.0)
            / jnp.maximum(4.0 * lower_deg * lower_deg - 1.0, 1.0)
        )
        recurred = upward * (cosine * previous - backward * before_prev)
        fresh_row = jnp.where(
            degree < orders[:, None], 0.0, jnp.where(degree == orders[:, None], seed_row, recurred)
        )
        return ((fresh_row, previous), fresh_row * unscale)

    zero_rows = jnp.zeros(seed_row.shape, jnp.float32)
    _, table_rows = lax.scan(
        advance, (zero_rows, zero_rows), jnp.arange(degrees, dtype=jnp.int32), unroll=16
    )
    return jnp.transpose(table_rows, (1, 0, 2)).astype(jnp.bfloat16)


def fourier_table(lon_count, orders_count):
    longitude = jnp.arange(lon_count, dtype=jnp.int32)
    orders = jnp.arange(orders_count, dtype=jnp.int32)
    phase = (longitude[:, None] * orders[None, :] % lon_count).astype(jnp.float32) * (
        2.0 * math.pi / lon_count
    )
    return (jnp.stack([jnp.cos(phase), -jnp.sin(phase)], axis=1) / math.sqrt(lon_count)).astype(
        jnp.bfloat16
    )


def quad_weights(lat_count):
    lat_index = jnp.arange(lat_count, dtype=jnp.float32)
    colatitude = math.pi * (lat_index + 0.5) / lat_count
    return 2.0 * math.pi * jnp.sin(colatitude) / math.sqrt(lat_count)


def analyse(legendre, spectra, owned_orders, tile_rows):
    slot_count, degrees, lat_count = legendre.shape
    col_count = spectra.shape[2]

    def analyse_per_order(operands):
        table_row, column, order_now = operands
        tiles = []
        for tile_no in range(degrees // tile_rows):
            first_row = tile_no * tile_rows
            tile_table = table_row[first_row : first_row + tile_rows]
            tiles.append(
                lax.cond(
                    order_now < first_row + tile_rows,
                    lambda: jnp.dot(tile_table, column, preferred_element_type=jnp.float32),
                    lambda: jnp.zeros((tile_rows, col_count), jnp.float32),
                )
            )
        return jnp.concatenate(tiles, axis=0)

    return lax.map(analyse_per_order, (legendre, spectra, owned_orders))


def synthesise(legendre, spectra, owned_orders, tile_rows):
    slot_count, degrees, lat_count = legendre.shape
    col_count = spectra.shape[2]

    def synthesise_per_order(operands):
        table_row, column, order_now = operands
        summed = jnp.zeros((lat_count, col_count), jnp.float32)
        for tile_no in range(degrees // tile_rows):
            first_row = tile_no * tile_rows
            tile_table = table_row[first_row : first_row + tile_rows]
            tile_spec = column[first_row : first_row + tile_rows]
            summed = summed + lax.cond(
                order_now < first_row + tile_rows,
                lambda: lax.dot_general(
                    tile_table,
                    tile_spec,
                    (((0,), (0,)), ((), ())),
                    preferred_element_type=jnp.float32,
                ),
                lambda: jnp.zeros((lat_count, col_count), jnp.float32),
            )
        return summed

    return lax.map(synthesise_per_order, (legendre, spectra, owned_orders))


def mix_down(spectra, real_weight, imaginary_weight):
    real_gradient = spectra[..., 0, :]
    imaginary_gradient = spectra[..., 1, :]
    mixed_real_part = jnp.einsum(
        "...lo,lco->...lc", real_gradient, real_weight, preferred_element_type=jnp.float32
    ) + jnp.einsum(
        "...lo,lco->...lc", imaginary_gradient, imaginary_weight, preferred_element_type=jnp.float32
    )
    mixed_imaginary_part = jnp.einsum(
        "...lo,lco->...lc", imaginary_gradient, real_weight, preferred_element_type=jnp.float32
    ) - jnp.einsum(
        "...lo,lco->...lc", real_gradient, imaginary_weight, preferred_element_type=jnp.float32
    )
    return jnp.stack([mixed_real_part, mixed_imaginary_part], axis=-2)


def shards(inputs, cotangent, weight):
    n_lat = lax.axis_size("lat")
    n_dp = lax.axis_size("dp")
    lat_rank = lax.axis_index("lat")
    samples, lat_dev, chan_dev, lon_count = inputs.shape
    lat_count = lat_dev * n_lat
    degrees = L
    per_owner = degrees // n_lat
    fourier = fourier_table(lon_count, degrees)
    quad_w = quad_weights(lat_count)
    local_quad = lax.dynamic_slice_in_dim(quad_w, lat_rank * lat_dev, lat_dev, 0)
    spec_in = (
        jnp.einsum("jck,krm->mjrc", inputs[0], fourier, preferred_element_type=jnp.float32)
        * local_quad[None, :, None, None]
    )
    spec_out = jnp.einsum(
        "jck,krm->mjrc", cotangent[0], fourier, preferred_element_type=jnp.float32
    )
    outgoing = (
        jnp.concatenate([spec_in, spec_out], axis=2)
        .astype(jnp.bfloat16)
        .reshape(degrees, lat_dev, 4 * chan_dev)
    )
    slot_index = jnp.arange(per_owner, dtype=jnp.int32)
    owned_orders = lat_rank * per_owner + slot_index
    arrived = lax.all_to_all(outgoing, "lat", split_axis=0, concat_axis=1, tiled=True)
    legendre = legendre_table(owned_orders, lat_count, degrees)
    tile_rows = degrees // 4
    analysed = analyse(legendre, arrived, owned_orders, tile_rows)
    coeffs = (
        analysed[:, :, : 2 * chan_dev]
        .astype(jnp.bfloat16)
        .reshape(1, per_owner, degrees, 2, chan_dev)
    )
    factor = jnp.where(owned_orders == 0, 1.0, 2.0) / math.sqrt(lat_count)
    grad_part = (
        (analysed[:, :, 2 * chan_dev :] * factor[:, None, None])
        .astype(jnp.bfloat16)
        .reshape(1, per_owner, degrees, 2, chan_dev)
    )
    grad_spec = lax.all_gather(grad_part, "lon", axis=4, tiled=True)
    coeff_deg, grad_deg = (
        lax.all_to_all(
            lax.all_to_all(coeffs, "lat", split_axis=2, concat_axis=1, tiled=True),
            "dp",
            split_axis=2,
            concat_axis=0,
            tiled=True,
        ),
        lax.all_to_all(
            lax.all_to_all(grad_spec, "lat", split_axis=2, concat_axis=1, tiled=True),
            "dp",
            split_axis=2,
            concat_axis=0,
            tiled=True,
        ),
    )
    rotated = jnp.stack([grad_deg[:, :, :, 1], -grad_deg[:, :, :, 0]], axis=3)
    weight_grad = jnp.stack(
        [
            jnp.einsum("smlrc,smlro->lco", coeff_deg, grad_deg, preferred_element_type=jnp.float32),
            jnp.einsum("smlrc,smlro->lco", coeff_deg, rotated, preferred_element_type=jnp.float32),
        ],
        axis=1,
    ) / (samples * n_dp)
    w_piece = lax.all_gather(weight, ("lat", "dp"), axis=0, tiled=True)
    grad_rows = grad_spec[0]
    mixed_spec = mix_down(grad_rows, w_piece[:, 0], w_piece[:, 1]).astype(jnp.bfloat16)
    synthesised = synthesise(
        legendre, mixed_spec.reshape(per_owner, degrees, 2 * chan_dev), owned_orders, tile_rows
    )
    outgoing_grid = (synthesised * quad_w[None, :, None]).astype(jnp.bfloat16)
    returned_grid = lax.all_to_all(outgoing_grid, "lat", split_axis=1, concat_axis=0, tiled=True)
    grad_field = jnp.einsum(
        "mjrc,krm->jck",
        returned_grid.reshape(degrees, lat_dev, 2, chan_dev),
        fourier,
        preferred_element_type=jnp.float32,
    ).astype(jnp.bfloat16)
    return (grad_field[None], weight_grad)


def solution(mesh):
    return jax.shard_map(
        shards,
        mesh=mesh,
        in_specs=(
            P("dp", "lat", "lon", None),
            P("dp", "lat", "lon", None),
            P(("lat", "dp"), None, "lon", None),
        ),
        out_specs=(P("dp", "lat", "lon", None), P(("lat", "dp"), None, "lon", None)),
        check_vma=False,
    )
```

profile of v0, /device:TPU:18, one launch (start us, length us, event | category | flops | bytes accessed | tf_op | source)
XLA Modules:
  0.0 1540.4 jit_solution(16707908449635445523)
XLA Ops:
  22.0 7.0 copy.93
  29.0 11.4 all-to-all-start
  42.1 582.7 %while.43 = (s32[]{:T(128)}, f32[24,384]{1,0:T(8,128)S(1)}, f32[24,384]{1,0:T(8,128)S(1)}, bf16[24,16,24,384]{3,2,1,0:T(8,128)(2,1)}, s32[24,16]{0,1:T(8,128)S(1...) while((s32[]{:T(128)}, f32[24,384]{1,0:T(8,128)S(1)}, ...), condition=%wide.region_4.5_spmd.clone.clone.clone.clone, body=%wide.region_3.4_spmd.clone.clone.clone.clone.sunk | while | flops 2097617 | bytes 3069356 | solution.py:51
  624.8 7.2 copy.134
  637.1 166.5 %while.41 = (s32[]{:T(128)}, f32[24,384,256]{1,2,0:T(8,128)}, s32[24]{0:T(128)S(1)}, bf16[24,384,384]{2,1,0:T(8,128)(2,1)}, bf16[24,384,256]{2,1,0:T(8,128)(2,1)...) while((s32[]{:T(128)}, f32[24,384,256]{1,2,0:T(8,128)}, s32[24]{0:T(128)S(1)}, ...), condition=%wide.region_14.15_spmd, body=%wide.region_5.14_spmd.sunk | while | flops 75792384 | bytes 4817633 | solution.py:93
  812.9 8.6 copy.105
  821.5 7.9 reshape.1049
  834.3 90.2 %all-gather.3.cloned.1.call-done = bf16[1,24,384,2,128]{2,1,3,0,4:T(8,128)(2,1)} async-done(((bf16[1,24,384,2,64]{2,1,3,0,4:T(8,128)(2,1)}), bf16[1,24,384,2,128]{2,1,3,0,4:T(8,128)(2,1)}) %all-gather.3.cloned.1.call-update) | async-done | bytes 4718608 | tf_op jit(solution)/shard_map/all_gather | solution.py:178
  924.5 7.6 copy.109
  932.1 9.1 all-to-all-start.4
  953.4 6.4 copy.108
  959.8 7.5 copy.97
  967.3 92.5 %all-to-all-done.4 = bf16[1,24,384,2,128]{4,1,3,0,2:T(8,128)(2,1)} async-done(((bf16[1,24,384,2,128]{4,1,3,0,2:T(8,128)(2,1)}), bf16[1,24,384,2,128]{4,1,3,0,2:T(8,128)(2,1)}, u32[]{:S(2)}, u32[]{:S(2)}) %all-to-all-start.4) | async-done | bytes 4718624 | tf_op jit(solution)/shard_map/all_to_all | solution.py:188
  1071.5 9.7 copy.112
  1081.2 14.8 all-gather.5.cloned.1.call-done
  1096.0 9.1 fusion.125
  1105.1 7.2 fusion.124
  1112.4 6.7 fusion.135
  1119.1 7.9 fusion.136
  1131.9 6.4 copy.99
  1139.7 6.7 all-to-all-start.5
  1146.4 302.8 %while.42 = (s32[]{:T(128)}, f32[24,384,128]{2,0,1:T(8,128)}, s32[24]{0:T(128)S(1)}, bf16[24,384,384]{2,1,0:T(8,128)(2,1)}, bf16[24,384,128]{1,2,0:T(8,128)(2,1)...) while((s32[]{:T(128)}, f32[24,384,128]{2,0,1:T(8,128)}, ...), condition=%wide.region_24.25_spmd, body=%wide.region_15.24_spmd.sunk | while | flops 37896196 | bytes 3539181 | solution.py:119
  1152.6 6.4 dynamic_update_slice.26
  1165.3 6.4 dynamic_update_slice.26
  1177.9 6.4 dynamic_update_slice.26
  1190.6 6.4 dynamic_update_slice.26
  1203.2 6.4 dynamic_update_slice.26
  1215.9 6.4 dynamic_update_slice.26
  1228.6 6.4 dynamic_update_slice.26
  1241.2 6.4 dynamic_update_slice.26
  1253.9 6.4 dynamic_update_slice.26
  1266.5 6.4 dynamic_update_slice.26
  1279.0 6.4 dynamic_update_slice.26
  1291.6 6.4 dynamic_update_slice.26
  1304.2 6.4 dynamic_update_slice.26
  1316.8 6.4 dynamic_update_slice.26
  1329.4 6.4 dynamic_update_slice.26
  1354.5 6.4 dynamic_update_slice.26
  1367.1 6.4 dynamic_update_slice.26
  1379.8 6.4 dynamic_update_slice.26
  1392.4 6.4 dynamic_update_slice.26
  1405.0 6.4 dynamic_update_slice.26
  1417.6 6.4 dynamic_update_slice.26
  1430.2 6.4 dynamic_update_slice.26
  1442.8 6.4 dynamic_update_slice.26
  1466.7 45.3 %all-to-all-done.1 = bf16[24,384,128]{2,0,1:T(8,128)(2,1)} async-done(((bf16[24,384,128]{2,0,1:T(8,128)(2,1)}), bf16[24,384,128]{2,0,1:T(8,128)(2,1)}, u32[]{:S(2)}, u32[]{:S(2)}) %all-to-all-start.1) | async-done | bytes 2359328 | tf_op jit(solution)/shard_map/all_to_all | solution.py:210
  1515.5 9.3 reshape.1028
  1524.8 8.5 fusion.137
  (1949 shorter events, 644.9 us)
Async XLA Ops:
  7.2 5.7 copy-start
  12.8 3.8 copy-start.5
  12.9 3.7 copy-start.7
  12.9 3.7 copy-start.9
  29.0 603.0 %all-to-all-start = ((bf16[384,24,256]{2,1,0:T(8,128)(2,1)}), bf16[384,24,256]{2,1,0:T(8,128)(2,1)}, u32[]{:S(2)}, u32[]{:S(2)}) async-start(bf16[384,24,256]{2,1,0:T(8,128)(2,1)} %copy.93), calls=%async_computation | async-start | bytes 9437184 | tf_op jit(solution)/shard_map/all_to_all | solution.py:163
  40.5 884.0 %all-gather.3.cloned.1.call-start = ((), (), s32[]{:S(2)}) async-start(), calls=%async_computation.6 | async-start | bytes 7077888 | tf_op jit(solution)/shard_map/all_gather | solution.py:178
  806.6 2.9 copy-start.8
  809.4 286.6 %all-gather.5.cloned.1.call-start = ((), (), s32[]{:S(2)}) async-start(), calls=%async_computation.7 | async-start | bytes 12681216 | tf_op jit(solution)/shard_map/all_gather | solution.py:203
  829.4 102.6 %all-to-all-start.2 = ((bf16[16,2,36864]{2,1,0:T(2,128)(2,1)}), bf16[16,2,36864]{2,1,0:T(2,128)(2,1)S(1)}, u32[]{:S(2)}, u32[]{:S(2)}) async-start(bf16[16,2,36864]{2,1,0:T(2,128)(2,1)} %reshape.1049), calls=%async_computation.2 | async-start | bytes 4718592 | tf_op jit(solution)/shard_map/all_to_all | solution.py:181
  932.1 127.7 %all-to-all-start.4 = ((bf16[1,24,384,2,128]{4,1,3,0,2:T(8,128)(2,1)}), bf16[1,24,384,2,128]{4,1,3,0,2:T(8,128)(2,1)}, u32[]{:S(2)}, u32[]{:S(2)}) async-start(bf16[1,24,384,2,128]{4,1,3,0,2:T(8,128)(2,1)} %copy.109), calls=%async_computation.4 | async-start | bytes 9437184 | tf_op jit(solution)/shard_map/all_to_all | solution.py:188
  1059.8 78.5 %all-to-all-start.3 = ((bf16[1,384,24,2,64]{1,4,3,0,2:T(8,128)(2,1)}), bf16[1,384,24,2,64]{1,4,3,0,2:T(8,128)(2,1)S(1)}, u32[]{:S(2)}, u32[]{:S(2)}) async-start(bf16[1,384,24,2,64]{1,4,3,0,2:T(8,128)(2,1)} %copy.108), calls=%async_computation.3 | async-start | bytes 4718592 | tf_op jit(solution)/shard_map/all_to_all | solution.py:180
  1096.0 9.1 copy-start.2
  1138.3 1.4 copy-start.3
  1139.7 313.7 %all-to-all-start.5 = ((bf16[1,384,24,2,128]{4,3,1,0,2:T(2,128)(2,1)}), bf16[1,384,24,2,128]{4,3,1,0,2:T(2,128)(2,1)}, u32[]{:S(2)}, u32[]{:S(2)}) async-start(bf16[1,384,24,2,128]{4,3,1,0,2:T(2,128)(2,1)} %copy.112), calls=%async_computation.5 | async-start | bytes 9437184 | tf_op jit(solution)/shard_map/all_to_all | solution.py:187
  1453.4 58.5 %all-to-all-start.1 = ((bf16[24,384,128]{2,0,1:T(8,128)(2,1)}), bf16[24,384,128]{2,0,1:T(8,128)(2,1)}, u32[]{:S(2)}, u32[]{:S(2)}) async-start(bf16[24,384,128]{2,0,1:T(8,128)(2,1)} %multiply_convert_fusion), calls=%async_computation.1 | async-start | bytes 4718592 | tf_op jit(solution)/shard_map/all_to_all | solution.py:210
  1462.2 1.7 copy-start.4
  1515.5 9.3 copy-start.6
  1515.5 17.8 %copy-start.1 = (bf16[1,24,64,768]{3,2,1,0:T(8,128)(2,1)S(1)}, bf16[1,24,64,768]{3,2,1,0:T(8,128)(2,1)}, u32[]{:S(2)}) copy-start(bf16[1,24,64,768]{3,2,1,0:T(8,128)(2,1)} %param.26) | copy-start | bytes 7077892
Sparse Core Ops, SparseCore 0:
  809.5 114.9 all-gather.2
  928.4 167.5 all-gather.4
where the time goes:
time: 1570 us; the launch traced here: 1540 us
  local copies, waits for them, and re-layouts  456 us (29%)
  loops' own time  386 us (25%)
  other arithmetic  314 us (20%)
  waiting for transfers between devices  243 us (15%)
  matrix products  83.7 us (5%)
  starting transfers between devices  42.6 us (3%)
    another operation x1, loops' own time, legendre_table(): lax.scan(advance, (zero_rows, zero_rows), jnp.arange(degrees, dtype=jnp.i...  255 us
    eq x384, other arithmetic, advance(): degree == orders[:, None]  245 us
    dynamic_update_slice x24, local copies, waits for them, and re-layouts, synthesise(): return lax.map(synthesise_per_order, (legendre, spectra, owned_orders))  154 us
    all_to_all x1, waiting for transfers between devices, shards(): lax.all_to_all(grad_spec, 'lat', split_axis=2, concat_axis=1, tiled=True)  92.5 us
    all_gather x1, waiting for transfers between devices, shards(): grad_spec = lax.all_gather(grad_part, 'lon', axis=4, tiled=True)  90.2 us
    dynamic_slice x96, local copies, waits for them, and re-layouts, analyse(): return lax.map(analyse_per_order, (legendre, spectra, owned_orders))  75.8 us
    another operation x1, loops' own time, synthesise(): return lax.map(synthesise_per_order, (legendre, spectra, owned_orders))  64.1 us
    another operation x1, loops' own time, analyse(): return lax.map(analyse_per_order, (legendre, spectra, owned_orders))  63.9 us
  transfers between devices with their start and end apart: 8, of which 4 were waited for; matrix products, arithmetic and copies ran while one was open for 45% of the time, Pallas kernels for 0%

commit v1 on v0

v1 whole, which is shorter than its diff:
```python
import math

import jax
import jax.numpy as jnp
import numpy as np
from jax import lax
from jax.experimental import pallas as pl
from jax.experimental.pallas import tpu as pltpu
from jax.sharding import Mesh
from jax.sharding import PartitionSpec as P

L = 384
NLON = 768
NLAT = 384
C = 128
OWNERS = 32
SLOTS = 12
JD = 24
PAIR_ROWS = 96
MIB = 1024 * 1024
F32 = jnp.float32
BF16 = jnp.bfloat16
ORDER_AXES = ("zh", "y", "lon")
DEGREE_AXES = ("y", "dp")


def order_of(owner, slot):
    half = slot // 2
    return 64 * half + owner if slot % 2 == 0 else 64 * half + 63 - owner


def pair_index():
    table, count = {}, 0
    for slot in range(SLOTS):
        for group in range(slot // 3, 4):
            for i in range(3):
                table[slot, group, i] = count
                count += 1
    return table


PAIRS = pair_index()


def fourier_rows():
    orders = np.array([order_of(o, k) for o in range(OWNERS) for k in range(SLOTS)], np.int64)
    phase = (orders[:, None] * np.arange(NLON)[None, :] % NLON) * (2.0 * math.pi / NLON)
    rows = np.concatenate([np.cos(phase), -np.sin(phase)], axis=0) / math.sqrt(NLON)
    return rows.astype(np.float32).astype(jnp.bfloat16)


def params(limit):
    return pltpu.CompilerParams(vmem_limit_bytes=limit * MIB)


def vmem_spec():
    return pl.BlockSpec(memory_space=pltpu.VMEM)


def low_half(shape):
    return lax.broadcasted_iota(jnp.int32, shape, len(shape) - 1) < 64


def dft_kernel(x_ref, table_ref, scale_ref, out_ref, held):
    step = pl.program_id(0)
    x = x_ref[...].reshape(128, NLON)
    spec = lax.dot_general(
        table_ref[...], x, (((1,), (1,)), ((), ())), preferred_element_type=F32
    )
    real, imag = spec[:L], spec[L:]
    low = low_half((L, 128))
    even = jnp.where(low, real, pltpu.roll(imag, 64, 1))
    odd = jnp.where(low, pltpu.roll(real, 64, 1), imag)
    scale = scale_ref[...]
    held[pl.ds(2 * step, L, stride=JD), :] = even * scale[0]
    held[pl.ds(2 * step + 1, L, stride=JD), :] = odd * scale[1]

    @pl.when(step == JD // 2 - 1)
    def _():
        def body(o, _):
            start = pl.multiple_of(o * 288, 288)
            out_ref[o] = held[pl.ds(start, 288), :].astype(BF16)
            return 0

        lax.fori_loop(0, OWNERS, body, 0)


def dft(x, table, scale):
    return pl.pallas_call(
        dft_kernel,
        grid=(JD // 2,),
        in_specs=[
            pl.BlockSpec((2, 64, NLON), lambda s: (s, 0, 0)),
            pl.BlockSpec((2 * L, NLON), lambda s: (0, 0)),
            pl.BlockSpec((2, 1, 128), lambda s: (s, 0, 0)),
        ],
        out_specs=pl.BlockSpec((OWNERS, 288, 128), lambda s: (0, 0, 0)),
        out_shape=jax.ShapeDtypeStruct((OWNERS, 288, 128), BF16),
        scratch_shapes=[pltpu.VMEM((L * JD, 128), F32)],
        compiler_params=params(40),
        cost_estimate=pl.CostEstimate(
            flops=2 * 1536 * 768 * 768, bytes_accessed=6_000_000, transcendentals=0
        ),
        name="dft",
    )(x, table, scale)


def legendre_kernel(order_ref, seed_ref, unscale_ref, cos_ref, up_ref, down_ref, out_ref, held):
    order = order_ref[...]
    cosine = cos_ref[...]

    def advance(degree, row, previous, before):
        up = up_ref[degree]
        down = down_ref[degree]
        fresh = []
        for c in range(3):
            lanes = slice(128 * c, 128 * c + 128)
            value = up * (cosine[:, lanes] * previous[c] - down * before[c])
            value = jnp.where(order == degree, seed_ref[:, lanes], value)
            value = jnp.where(order > degree, 0.0, value)
            held[c, pl.ds(row, 16, stride=L), :] = value * unscale_ref[:, lanes]
            fresh.append(value)
        return fresh, previous

    def body(step, carry):
        previous, before = list(carry[:3]), list(carry[3:])
        group = step // 32
        d = step - 32 * group
        for i in range(3):
            previous, before = advance(3 * step + i, 96 * group + 32 * i + d, previous, before)
        return tuple(previous) + tuple(before)

    zero = jnp.zeros((16, 128), F32)
    lax.fori_loop(0, L // 3, body, (zero,) * 6)

    def convert(k, _):
        start = pl.multiple_of(k * L, L)
        for c in range(3):
            out_ref[pl.ds(start, L), 128 * c : 128 * c + 128] = held[
                c, pl.ds(start, L), :
            ].astype(BF16)
        return 0

    lax.fori_loop(0, SLOTS, convert, 0)


def legendre(owner):
    lat_index = jnp.arange(NLAT, dtype=F32)
    colatitude = math.pi * (lat_index + 0.5) / NLAT
    cosine = jnp.cos(colatitude)[None, :]
    sine_v = jnp.sin(colatitude)[None, :]
    slots = jnp.arange(16, dtype=jnp.int32)
    orders = jnp.where(slots % 2 == 0, 64 * (slots // 2) + owner, 64 * (slots // 2) + 63 - owner)
    orders = jnp.minimum(orders, L - 1)
    step_nums = np.arange(1, L, dtype=np.float64)
    cumlog = np.concatenate([np.zeros(1), np.cumsum(np.log1p(-0.5 / step_nums))]).astype(np.float32)
    selector = (orders[:, None] == jnp.arange(L, dtype=jnp.int32)[None, :]).astype(F32)
    order_log = jnp.sum(selector * cumlog[None, :], axis=1)
    order_f = orders.astype(F32)[:, None]
    log_start = 0.5 * (
        jnp.log(2.0 * order_f + 1.0) - math.log(4.0 * math.pi) + order_log[:, None]
    ) + order_f * jnp.log(sine_v)
    shift_up = jnp.clip(-log_start - 60.0, 0.0, 80.0)
    seed_row = jnp.exp(log_start + shift_up)
    unscale = jnp.exp(-shift_up)
    degree_f = jnp.arange(L, dtype=F32)[:, None]
    order_g = orders.astype(F32)[None, :]
    upward = jnp.sqrt(
        jnp.maximum(4.0 * degree_f * degree_f - 1.0, 1.0)
        / jnp.maximum(degree_f * degree_f - order_g * order_g, 1.0)
    )
    lower = degree_f - 1.0
    backward = jnp.sqrt(
        jnp.maximum(lower * lower - order_g * order_g, 0.0)
        / jnp.maximum(4.0 * lower * lower - 1.0, 1.0)
    )
    wide = (L, 16, 128)
    return pl.pallas_call(
        legendre_kernel,
        in_specs=[vmem_spec()] * 6,
        out_specs=vmem_spec(),
        out_shape=jax.ShapeDtypeStruct((SLOTS * L, NLAT), BF16),
        scratch_shapes=[pltpu.VMEM((3, 16 * L, 128), F32)],
        compiler_params=params(48),
        cost_estimate=pl.CostEstimate(
            flops=10 * 16 * 384 * 384, bytes_accessed=10_000_000, transcendentals=0
        ),
        name="legendre",
    )(
        jnp.broadcast_to(orders[:, None], (16, 128)),
        seed_row,
        unscale,
        jnp.broadcast_to(cosine, (16, NLAT)),
        jnp.broadcast_to(upward[:, :, None], wide),
        jnp.broadcast_to(backward[:, :, None], wide),
    )


def widen(src_ref, held, rows):
    def body(o, _):
        start = pl.multiple_of(o * rows, rows)
        held[pl.ds(start, rows), :] = src_ref[o].astype(F32)
        return 0

    lax.fori_loop(0, OWNERS, body, 0)


def narrow(held, out_ref, rows):
    def body(o, _):
        start = pl.multiple_of(o * rows, rows)
        out_ref[o] = held[pl.ds(start, rows), :].astype(BF16)
        return 0

    lax.fori_loop(0, OWNERS, body, 0)


def analyse_kernel(spec_ref, table_ref, factor_ref, out_ref, field, packed):
    widen(spec_ref, field, 288)
    packed[...] = jnp.zeros_like(packed)
    for k in range(SLOTS):
        first = k // 3
        columns = []
        for lon in range(2):
            pieces = [
                field[(2 * s + lon) * 288 + k * JD : (2 * s + lon) * 288 + k * JD + JD, :]
                for s in range(16)
            ]
            columns.append(jnp.concatenate(pieces, axis=0).astype(BF16))
        data = jnp.concatenate(columns, axis=1)
        rows = table_ref[k * L + 96 * first : (k + 1) * L, :]
        result = jnp.dot(rows, data, preferred_element_type=F32) * factor_ref[k : k + 1, :]
        for group in range(first, 4):
            for i in range(3):
                at = ((group - first) * 3 + i) * 32
                for lon in range(2):
                    row = lon * PAIR_ROWS + PAIRS[k, group, i]
                    packed[pl.ds(row, 32, stride=192), :] = result[
                        at : at + 32, 128 * lon : 128 * lon + 128
                    ]
    narrow(packed, out_ref, 192)


def analyse(spec, table, factor, name):
    return pl.pallas_call(
        analyse_kernel,
        in_specs=[vmem_spec()] * 3,
        out_specs=vmem_spec(),
        out_shape=jax.ShapeDtypeStruct((OWNERS, 192, 128), BF16),
        scratch_shapes=[pltpu.VMEM((OWNERS * 288, 128), F32), pltpu.VMEM((OWNERS * 192, 128), F32)],
        compiler_params=params(48),
        cost_estimate=pl.CostEstimate(
            flops=2 * 12 * 384 * 384 * 256, bytes_accessed=8_000_000, transcendentals=0
        ),
        name=name,
    )(spec, table, factor)


def degree_rows(held, group, i):
    parts = []
    for lon in range(2):
        pieces = [
            held[pl.ds(lon * PAIR_ROWS + PAIRS[k, group, i], 32, stride=192), :]
            for k in range(3 * group + 3)
        ]
        parts.append(jnp.concatenate(pieces, axis=0).astype(BF16))
    return jnp.concatenate(parts, axis=1)


def mix_kernel(grad_ref, weight_ref, out_ref, held, packed):
    widen(grad_ref, held, 192)
    packed[...] = jnp.zeros_like(packed)
    for group in range(4):
        for i in range(3):
            rows = degree_rows(held, group, i)
            mixed = lax.dot_general(
                rows,
                weight_ref[group * 3 + i],
                (((1,), (1,)), ((), ())),
                preferred_element_type=F32,
            )
            for k in range(3 * group + 3):
                for lon in range(2):
                    row = lon * PAIR_ROWS + PAIRS[k, group, i]
                    packed[pl.ds(row, 32, stride=192), :] = mixed[
                        32 * k : 32 * k + 32, 128 * lon : 128 * lon + 128
                    ]
    narrow(packed, out_ref, 192)


def mix(grads, weights):
    return pl.pallas_call(
        mix_kernel,
        in_specs=[vmem_spec()] * 2,
        out_specs=vmem_spec(),
        out_shape=jax.ShapeDtypeStruct((OWNERS, 192, 128), BF16),
        scratch_shapes=[pltpu.VMEM((OWNERS * 192, 128), F32)] * 2,
        compiler_params=params(40),
        cost_estimate=pl.CostEstimate(
            flops=2 * 2880 * 256 * 256, bytes_accessed=5_000_000, transcendentals=0
        ),
        name="mix",
    )(grads, weights)


def weight_grad_kernel(coeff_ref, grad_ref, out_ref, held_c, held_g):
    widen(coeff_ref, held_c, 192)
    widen(grad_ref, held_g, 192)
    low = low_half((64, 128))
    for group in range(4):
        for i in range(3):
            coeffs = degree_rows(held_c, group, i)
            grads = degree_rows(held_g, group, i)
            product = lax.dot_general(
                coeffs, grads, (((0,), (0,)), ((), ())), preferred_element_type=F32
            ) * 0.125
            for lon in range(2):
                turned = []
                for half in range(2):
                    lanes = slice(128 * half, 128 * half + 128)
                    with_real = product[128 * lon : 128 * lon + 64, lanes]
                    with_imag = pltpu.roll(product[128 * lon + 64 : 128 * lon + 128, lanes], 64, 1)
                    turned.append(jnp.where(low, with_real + with_imag, with_real - with_imag))
                first, second = turned
                out_ref[2 * group + lon, 128 * i : 128 * i + 64, :] = jnp.where(
                    low, first, pltpu.roll(second, 64, 1)
                )
                out_ref[2 * group + lon, 128 * i + 64 : 128 * i + 128, :] = jnp.where(
                    low, pltpu.roll(first, 64, 1), second
                )


def weight_grads(coeffs, grads):
    return pl.pallas_call(
        weight_grad_kernel,
        in_specs=[vmem_spec()] * 2,
        out_specs=vmem_spec(),
        out_shape=jax.ShapeDtypeStruct((8, 384, 128), F32),
        scratch_shapes=[pltpu.VMEM((OWNERS * 192, 128), F32)] * 2,
        compiler_params=params(40),
        cost_estimate=pl.CostEstimate(
            flops=2 * 2880 * 256 * 256, bytes_accessed=5_000_000, transcendentals=0
        ),
        name="weight_grads",
    )(coeffs, grads)


def synthesise_kernel(mixed_ref, table_ref, quad_ref, out_ref, held, grid):
    widen(mixed_ref, held, 192)
    for k in range(SLOTS):
        first = k // 3
        parts = []
        for lon in range(2):
            pieces = [
                held[pl.ds(lon * PAIR_ROWS + PAIRS[k, group, i], 32, stride=192), :]
                for group in range(first, 4)
                for i in range(3)
            ]
            parts.append(jnp.concatenate(pieces, axis=0).astype(BF16))
        data = jnp.concatenate(parts, axis=1)
        rows = table_ref[k * L + 96 * first : (k + 1) * L, :]
        result = lax.dot_general(
            rows, data, (((0,), (0,)), ((), ())), preferred_element_type=F32
        )
        for lon in range(2):
            scaled = result[:, 128 * lon : 128 * lon + 128] * quad_ref[...]
            for s in range(16):
                at = (2 * s + lon) * 288 + k * JD
                grid[at : at + JD, :] = scaled[s * JD : s * JD + JD]
    narrow(grid, out_ref, 288)


def synthesise(mixed, table, quad):
    return pl.pallas_call(
        synthesise_kernel,
        in_specs=[vmem_spec()] * 3,
        out_specs=vmem_spec(),
        out_shape=jax.ShapeDtypeStruct((OWNERS, 288, 128), BF16),
        scratch_shapes=[pltpu.VMEM((OWNERS * 192, 128), F32), pltpu.VMEM((OWNERS * 288, 128), F32)],
        compiler_params=params(48),
        cost_estimate=pl.CostEstimate(
            flops=2 * 12 * 384 * 384 * 256, bytes_accessed=8_000_000, transcendentals=0
        ),
        name="synthesise",
    )(mixed, table, quad)


def inverse_kernel(spec_ref, table_ref, out_ref, held, turned):
    step = pl.program_id(0)

    @pl.when(step == 0)
    def _():
        widen(spec_ref, held, 288)

    for jj in range(4):
        block = held[pl.ds(4 * step + jj, L, stride=JD), :]
        flipped = jnp.transpose(block).astype(BF16)
        turned[64 * jj : 64 * jj + 64, :L] = flipped[:64]
        turned[64 * jj : 64 * jj + 64, L:] = flipped[64:]
    field = jnp.dot(turned[...], table_ref[...], preferred_element_type=F32)
    out_ref[...] = field.astype(BF16).reshape(4, 64, NLON)


def inverse(spec, table):
    return pl.pallas_call(
        inverse_kernel,
        grid=(JD // 4,),
        in_specs=[
            pl.BlockSpec((OWNERS, 288, 128), lambda s: (0, 0, 0)),
            pl.BlockSpec((2 * L, NLON), lambda s: (0, 0)),
        ],
        out_specs=pl.BlockSpec((4, 64, NLON), lambda s: (s, 0, 0)),
        out_shape=jax.ShapeDtypeStruct((JD, 64, NLON), BF16),
        scratch_shapes=[pltpu.VMEM((L * JD, 128), F32), pltpu.VMEM((256, 2 * L), BF16)],
        compiler_params=params(40),
        cost_estimate=pl.CostEstimate(
            flops=2 * 1536 * 768 * 768, bytes_accessed=6_000_000, transcendentals=0
        ),
        name="inverse_dft",
    )(spec, table)


def exchange(x, axes):
    return lax.all_to_all(x, axes, split_axis=0, concat_axis=0, tiled=True)


def mixing_matrices(gathered):
    w = gathered.reshape(4, 2, 3, 2, 64, 2, 64)
    real, imag = w[:, :, :, 0], w[:, :, :, 1]
    both = jnp.stack(
        [jnp.stack([real, imag], axis=5), jnp.stack([-imag, real], axis=5)], axis=3
    )
    return both.transpose(0, 2, 1, 3, 4, 5, 6, 7).reshape(12, 256, 256)


def shards(inputs, cotangent, weight):
    owner = (lax.axis_index("zh") * 4 + lax.axis_index("y")) * 2 + lax.axis_index("lon")
    lat_rank = lax.axis_index("zh") * 4 + lax.axis_index("y")
    table = jnp.asarray(fourier_rows())
    lat = np.arange(NLAT, dtype=np.float64)
    quad = (2.0 * math.pi * np.sin(math.pi * (lat + 0.5) / NLAT) / math.sqrt(NLAT)).astype(np.float32)
    quad = jnp.asarray(np.broadcast_to(quad[:, None], (NLAT, 128)))
    local_quad = lax.dynamic_slice_in_dim(quad, lat_rank * JD, JD, 0).reshape(JD, 1, 128)

    spec_out = exchange(dft(cotangent[0], table, jnp.ones((JD, 1, 128), F32)), ORDER_AXES)
    spec_in = exchange(dft(inputs[0], table, local_quad), ORDER_AXES)
    gathered = lax.all_gather(weight, ("zh", "lon"), axis=0, tiled=False)
    weights = mixing_matrices(gathered)
    legend = legendre(owner)

    base = 1.0 / math.sqrt(NLAT)
    factor = jnp.full((16, 256), 2.0 * base, F32)
    factor = factor.at[0].set(jnp.where(owner == 0, base, 2.0 * base))
    grads = exchange(analyse(spec_out, legend, factor, "analyse_grad"), DEGREE_AXES)
    mixed = exchange(mix(grads, weights), DEGREE_AXES)
    grid = exchange(synthesise(mixed, legend, quad), ORDER_AXES)
    coeffs = exchange(
        analyse(spec_in, legend, jnp.ones((16, 256), F32), "analyse_field"), DEGREE_AXES
    )
    partial = weight_grads(coeffs, grads)
    weight_grad = lax.psum_scatter(partial, ("zh", "lon"), scatter_dimension=0, tiled=False)
    field = inverse(grid, table)
    return field[None], weight_grad.reshape(3, 2, 64, 128)


def solution(mesh):
    fine = Mesh(mesh.devices.reshape(4, 4, 2, 8), ("zh", "y", "lon", "dp"))
    field = P("dp", ("zh", "y"), "lon", None)
    spectral = P(("zh", "y", "dp"), None, "lon", None)
    return jax.shard_map(
        shards,
        mesh=fine,
        in_specs=(field, field, spectral),
        out_specs=(field, spectral),
        check_vma=False,
    )
```

time: 1570 us -> 378 us (0.24); the launches traced: 1540 us -> 374 us
  local copies, waits for them, and re-layouts: 456 us -> 33.3 us
  loops' own time: 386 us -> 0 us
  other arithmetic: 314 us -> 2 us
  waiting for transfers between devices: 243 us -> 133 us
  matrix products: 83.7 us -> 0 us
  blocking collectives: 0 us -> 76.1 us
  Pallas kernels: 0 us -> 66.1 us
    another operation x195 -> x0, loops' own time: 386 us -> none  [the longest x1 255 us: legendre_table(): lax.scan(advance, (zero_rows, zero_rows), jnp.arange(degrees, dtype=jnp.i...]
    eq x384 -> x0, other arithmetic: 245 us -> none  [advance(): degree == orders[:, None]]
    dynamic_update_slice x96 -> x0, local copies, waits for them, and re-layouts: 195 us -> none  [the longest x24 154 us: synthesise(): return lax.map(synthesise_per_order, (legendre, spectra, owned_orders))]
    all_gather x2 -> x0, waiting for transfers between devices: 105 us -> none  [the longest x1 90.2 us: shards(): grad_spec = lax.all_gather(grad_part, 'lon', axis=4, tiled=True)]
    dynamic_slice x145 -> x1, local copies, waits for them, and re-layouts: 101 us -> 0.08 us  [shards(): lax.dynamic_slice_in_dim(quad, lat_rank * JD, JD, 0).reshape(JD, 1, 128)]
    dot_general x201 -> x0, matrix products: 83.7 us -> none  [the longest x96 19.6 us: synthesise_per_order(): lax.dot_general(tile_table, tile_spec, (((0,), (0,)), ((), ())), preferre...]
    all_gather x0 -> x1, blocking collectives: none -> 76.1 us  [shards(): gathered = lax.all_gather(weight, ('zh', 'lon'), axis=0, tiled=False)]
    pallas_call x0 -> x9, Pallas kernels: none -> 66.1 us  [the longest x1 15.2 us: legendre(): pl.pallas_call(legendre_kernel, in_specs=[vmem_spec()] * 6, out_specs=vme...]
  transfers between devices with their start and end apart: 8 -> 7, of which waited for: 4 -> 5; matrix products, arithmetic and copies ran while one was open for 45% -> 6% of each run, Pallas kernels for 0% -> 14%
where the time goes in v1:
time: 378 us; the launch traced here: 374 us
  waiting for transfers between devices  133 us (35%)
  blocking collectives  76.1 us (20%)
  Pallas kernels  66.1 us (17%)
  starting transfers between devices  49.5 us (13%)
  local copies, waits for them, and re-layouts  33.3 us (9%)
  between operations  14.4 us (4%)
    all_to_all x6, waiting for transfers between devices, exchange(): return lax.all_to_all(x, axes, split_axis=0, concat_axis=0, tiled=True)  133 us
    all_gather x1, blocking collectives, shards(): gathered = lax.all_gather(weight, ('zh', 'lon'), axis=0, tiled=False)  76.1 us
    all_to_all x6, starting transfers between devices, exchange(): return lax.all_to_all(x, axes, split_axis=0, concat_axis=0, tiled=True)  49.5 us
    pallas_call x1, Pallas kernels, legendre(): pl.pallas_call(legendre_kernel, in_specs=[vmem_spec()] * 6, out_specs=vme...  15.2 us
    pallas_call x2, Pallas kernels, dft(): pl.pallas_call(dft_kernel, grid=(JD // 2,), in_specs=[pl.BlockSpec((2, 64...  13.8 us
    unnamed x30, local copies, waits for them, and re-layouts  13.7 us
    pallas_call x2, Pallas kernels, analyse(): pl.pallas_call(analyse_kernel, in_specs=[vmem_spec()] * 3, out_specs=vmem...  13.3 us
  transfers between devices with their start and end apart: 7, of which 5 were waited for; matrix products, arithmetic and copies ran while one was open for 6% of the time, Pallas kernels for 14%

profile of v1, /device:TPU:18, one launch (start us, length us, event | category | flops | bytes accessed | tf_op | source)
XLA Modules:
  0.0 374.0 jit_solution(16755358271344737425)
XLA Ops:
  7.2 1.7 copy-done.7
  8.8 1.3 copy-done.9
  10.1 6.9 %dft.2 = bf16[32,288,128]{2,1,0:T(8,128)(2,1)S(1)} custom-call(bf16[24,64,768]{2,1,0:T(8,128)(2,1)S(1)} %bitcast.19, bf16[768,768]{1,0:T(8,128)(2,1)S(1)} %copy-done.9, f32[24,1,128]{2,1,0:T(1,128)S(1)} %broadcast_in_dim.14.scale_ref), custom_call_target="tpu_custom_call" | custom-call | flops 1811939328 | bytes 6000000 | tf_op jit(solution)/shard_map/dft/pallas_call | solution.py:89
  17.0 1.4 copy-done.5
  18.4 11.7 %all-to-all-start = ((bf16[32,288,128]{2,1,0:T(8,128)(2,1)}), bf16[32,288,128]{2,1,0:T(8,128)(2,1)S(1)}, u32[]{:S(2)}, u32[]{:S(2)}) async-start(bf16[32,288,128]{2,1,0:T(8,128)(2,1)} %copy-done.5), calls=%async_computation | async-start | bytes 4718592 | tf_op jit(solution)/shard_map/all_to_all | solution.py:423
  30.2 0.2 select_reduce_fusion
  30.4 0.1 divide_sqrt_fusion
  30.5 0.1 copy.18
  30.7 0.1 copy.19
  30.9 0.1 negate_exponential_fusion
  31.0 0.9 broadcast_in_dim.17.up_ref
  31.9 2.2 broadcast_in_dim.18.down_ref
  34.1 15.2 %legendre.1.table_ref = bf16[4608,384]{1,0:T(8,128)(2,1)} custom-call(s32[16,128]{1,0:T(8,128)S(1)} %broadcast_in_dim.15.order_ref, f32[16,384]{1,0:T(8,128)S(1)} %get-tuple-element.19.seed_ref, f32[16,384]{1,0:T(8,128)S(1)} %get-tuple-element.18.unscale_ref, f32[16,384]{1,0:T(8,128)S(1)} %broadcast_in_dim.16.cos_ref, ...), custom_call_target="tpu_custom_call" | custom-call | flops 23592960 | bytes 10000000 | tf_op jit(solution)/shard_map/legendre/pallas_call | solution.py:178
  49.3 37.0 %all-to-all-done.spec_ref = bf16[32,288,128]{2,1,0:T(8,128)(2,1)S(1)} async-done(((bf16[32,288,128]{2,1,0:T(8,128)(2,1)}), bf16[32,288,128]{2,1,0:T(8,128)(2,1)S(1)}, u32[]{:S(2)}, u32[]{:S(2)}) %all-to-all-start) | async-done | bytes 2359328 | tf_op jit(solution)/shard_map/all_to_all | solution.py:423
  86.4 5.7 %analyse_grad.1 = bf16[32,192,128]{2,1,0:T(8,128)(2,1)S(1)} custom-call(bf16[32,288,128]{2,1,0:T(8,128)(2,1)S(1)} %all-to-all-done.spec_ref, bf16[4608,384]{1,0:T(8,128)(2,1)} %legendre.1.table_ref, f32[16,256]{1,0:T(8,128)S(1)} %scatter.8.factor_ref), custom_call_target="tpu_custom_call" | custom-call | flops 905969664 | bytes 8000000 | tf_op jit(solution)/shard_map/analyse_grad/pallas_call | solution.py:244
  92.1 1.2 copy-done.1
  93.3 7.5 %all-to-all-start.1 = ((bf16[32,192,128]{2,1,0:T(8,128)(2,1)}), bf16[32,192,128]{2,1,0:T(8,128)(2,1)S(1)}, u32[]{:S(2)}, u32[]{:S(2)}) async-start(bf16[32,192,128]{2,1,0:T(8,128)(2,1)} %copy-done.1), calls=%async_computation.1 | async-start | bytes 3145728 | tf_op jit(solution)/shard_map/all_to_all | solution.py:423
  100.9 0.1 broadcast.463.scale_ref
  101.0 1.7 copy-done.8
  102.7 6.9 %dft.3 = bf16[32,288,128]{2,1,0:T(8,128)(2,1)S(1)} custom-call(bf16[24,64,768]{2,1,0:T(8,128)(2,1)S(1)} %bitcast.20, bf16[768,768]{1,0:T(8,128)(2,1)S(1)} %copy-done.10, f32[24,1,128]{2,1,0:T(1,128)S(1)} %broadcast.463.scale_ref), custom_call_target="tpu_custom_call" | custom-call | flops 1811939328 | bytes 6000000 | tf_op jit(solution)/shard_map/dft/pallas_call | solution.py:89
  109.6 1.4 copy-done.6
  111.0 9.7 %all-to-all-done.1.grad_ref = bf16[32,192,128]{2,1,0:T(8,128)(2,1)S(1)} async-done(((bf16[32,192,128]{2,1,0:T(8,128)(2,1)}), bf16[32,192,128]{2,1,0:T(8,128)(2,1)S(1)}, u32[]{:S(2)}, u32[]{:S(2)}) %all-to-all-start.1) | async-done | bytes 1572896 | tf_op jit(solution)/shard_map/all_to_all | solution.py:423
  120.7 7.2 %all-to-all-start.4 = ((bf16[32,288,128]{2,1,0:T(8,128)(2,1)}), bf16[32,288,128]{2,1,0:T(8,128)(2,1)}, u32[]{:S(2)}, u32[]{:S(2)}) async-start(bf16[32,288,128]{2,1,0:T(8,128)(2,1)} %copy-done.6), calls=%async_computation.4 | async-start | bytes 4718592 | tf_op jit(solution)/shard_map/all_to_all | solution.py:423
  127.9 76.1 %all-gather = bf16[24,2,64,128]{3,2,1,0:T(8,128)(2,1)} all-gather(bf16[3,2,64,128]{3,2,1,0:T(8,128)(2,1)S(1)} %copy-done.12), channel_id=2, replica_groups=mesh['zh'=4,'y'=4,'lon'=2,'dp'=8] {'zh','lon'}, dimensions={0}, use_global_device_ids=true | all-gather | bytes 884736 | tf_op jit(solution)/shard_map/all_gather | solution.py:446
  204.0 3.2 reshape.258
  207.2 1.3 fusion.10
  208.5 0.2 fusion.9
  208.7 0.4 copy_bitcast_fusion
  209.1 0.6 maximum_bitcast_fusion.1
  209.7 0.7 maximum_bitcast_fusion
  210.5 4.9 %copy.22 = bf16[4,3,2,2,64,2,2,64]{7,6,5,4,3,2,1,0:T(2,128)(2,1)} copy(bf16[4,3,2,2,64,2,2,64]{7,4,6,5,1,2,0,3:T(8,128)(2,1)S(1)} %maximum_bitcast_fusion) | data formatting | bytes 3145728 | tf_op jit(solution)/shard_map/transpose | solution.py:432
  215.4 6.0 %reshape.259.weight_ref = bf16[12,256,256]{2,1,0:T(8,128)(2,1)S(1)} reshape(bf16[4,3,2,2,64,2,2,64]{7,6,5,4,3,2,1,0:T(2,128)(2,1)} %copy.22) | data formatting | bytes 3145728 | tf_op jit(solution)/shard_map/reshape | solution.py:432
  221.4 5.8 %mix.1 = bf16[32,192,128]{2,1,0:T(8,128)(2,1)} custom-call(bf16[32,192,128]{2,1,0:T(8,128)(2,1)S(1)} %all-to-all-done.1.grad_ref, bf16[12,256,256]{2,1,0:T(8,128)(2,1)S(1)} %reshape.259.weight_ref), custom_call_target="tpu_custom_call" | custom-call | flops 377487360 | bytes 5000000 | tf_op jit(solution)/shard_map/mix/pallas_call | solution.py:291
  227.2 6.4 %all-to-all-start.2 = ((bf16[32,192,128]{2,1,0:T(8,128)(2,1)}), bf16[32,192,128]{2,1,0:T(8,128)(2,1)S(1)}, u32[]{:S(2)}, u32[]{:S(2)}) async-start(bf16[32,192,128]{2,1,0:T(8,128)(2,1)} %mix.1), calls=%async_computation.2 | async-start | bytes 3145728 | tf_op jit(solution)/shard_map/all_to_all | solution.py:423
  233.7 7.6 %analyse_field.1 = bf16[32,192,128]{2,1,0:T(8,128)(2,1)} custom-call(bf16[32,288,128]{2,1,0:T(8,128)(2,1)} %all-to-all-done.4.spec_ref, bf16[4608,384]{1,0:T(8,128)(2,1)} %legendre.1.table_ref, f32[16,256]{1,0:T(8,128)S(1)} %broadcast_in_dim.20.factor_ref), custom_call_target="tpu_custom_call" | custom-call | flops 905969664 | bytes 8000000 | tf_op jit(solution)/shard_map/analyse_field/pallas_call | solution.py:244
  241.3 12.2 %all-to-all-done.2.mixed_ref = bf16[32,192,128]{2,1,0:T(8,128)(2,1)S(1)} async-done(((bf16[32,192,128]{2,1,0:T(8,128)(2,1)}), bf16[32,192,128]{2,1,0:T(8,128)(2,1)S(1)}, u32[]{:S(2)}, u32[]{:S(2)}) %all-to-all-start.2) | async-done | bytes 1572896 | tf_op jit(solution)/shard_map/all_to_all | solution.py:423
  253.5 1.1 copy-done.3
  254.7 8.1 %all-to-all-start.5 = ((bf16[32,192,128]{2,1,0:T(8,128)(2,1)}), bf16[32,192,128]{2,1,0:T(8,128)(2,1)S(1)}, u32[]{:S(2)}, u32[]{:S(2)}) async-start(bf16[32,192,128]{2,1,0:T(8,128)(2,1)} %analyse_field.1), calls=%async_computation.5 | async-start | bytes 3145728 | tf_op jit(solution)/shard_map/all_to_all | solution.py:423
  262.7 0.1 jit_solution_.3.quad_ref
  262.9 1.4 copy-done.4
  264.3 5.0 %synthesise.1 = bf16[32,288,128]{2,1,0:T(8,128)(2,1)S(1)} custom-call(bf16[32,192,128]{2,1,0:T(8,128)(2,1)S(1)} %copy-done.4, bf16[4608,384]{1,0:T(8,128)(2,1)} %legendre.1.table_ref, f32[384,128]{1,0:T(8,128)S(1)} %jit_solution_.3.quad_ref), custom_call_target="tpu_custom_call" | custom-call | flops 905969664 | bytes 8000000 | tf_op jit(solution)/shard_map/synthesise/pallas_call | solution.py:373
  269.2 1.4 copy-done
  270.6 11.9 %all-to-all-done.5.coeff_ref = bf16[32,192,128]{2,1,0:T(8,128)(2,1)S(1)} async-done(((bf16[32,192,128]{2,1,0:T(8,128)(2,1)}), bf16[32,192,128]{2,1,0:T(8,128)(2,1)S(1)}, u32[]{:S(2)}, u32[]{:S(2)}) %all-to-all-start.5) | async-done | bytes 1572896 | tf_op jit(solution)/shard_map/all_to_all | solution.py:423
  282.6 8.6 %all-to-all-start.3 = ((bf16[32,288,128]{2,1,0:T(8,128)(2,1)}), bf16[32,288,128]{2,1,0:T(8,128)(2,1)}, u32[]{:S(2)}, u32[]{:S(2)}) async-start(bf16[32,288,128]{2,1,0:T(8,128)(2,1)} %copy-done), calls=%async_computation.3 | async-start | bytes 4718592 | tf_op jit(solution)/shard_map/all_to_all | solution.py:423
  291.2 6.2 %weight_grads.1 = f32[8,384,128]{2,1,0:T(8,128)S(1)} custom-call(bf16[32,192,128]{2,1,0:T(8,128)(2,1)S(1)} %all-to-all-done.5.coeff_ref, bf16[32,192,128]{2,1,0:T(8,128)(2,1)S(1)} %all-to-all-done.1.grad_ref), custom_call_target="tpu_custom_call" | custom-call | flops 377487360 | bytes 5000000 | tf_op jit(solution)/shard_map/weight_grads/pallas_call | solution.py:333
  297.4 1.2 copy-done.2
  298.6 61.8 %all-to-all-done.3.spec_ref = bf16[32,288,128]{2,1,0:T(8,128)(2,1)} async-done(((bf16[32,288,128]{2,1,0:T(8,128)(2,1)}), bf16[32,288,128]{2,1,0:T(8,128)(2,1)}, u32[]{:S(2)}, u32[]{:S(2)}) %all-to-all-start.3) | async-done | bytes 2359328 | tf_op jit(solution)/shard_map/all_to_all | solution.py:423
  360.4 6.8 %inverse_dft.1 = bf16[24,64,768]{2,1,0:T(8,128)(2,1)} custom-call(bf16[32,288,128]{2,1,0:T(8,128)(2,1)} %all-to-all-done.3.spec_ref, bf16[768,768]{1,0:T(8,128)(2,1)S(1)} %copy-done.11), custom_call_target="tpu_custom_call" | custom-call | flops 1811939328 | bytes 6000000 | tf_op jit(solution)/shard_map/inverse_dft/pallas_call | solution.py:404
  (38 shorter events, 0.5 us)
Async XLA Ops:
  7.2 1.7 copy-start.7
  8.8 1.3 copy-start.9
  17.0 1.4 copy-start.5
  18.4 11.8 %copy-start.14 = (f32[384]{0:T(512)S(1)}, f32[384]{0:T(512)}, u32[]{:S(2)}) copy-start(f32[384]{0:T(512)} %constant.148) | copy-start | bytes 4612
  18.4 67.9 %all-to-all-start = ((bf16[32,288,128]{2,1,0:T(8,128)(2,1)}), bf16[32,288,128]{2,1,0:T(8,128)(2,1)S(1)}, u32[]{:S(2)}, u32[]{:S(2)}) async-start(bf16[32,288,128]{2,1,0:T(8,128)(2,1)} %copy-done.5), calls=%async_computation | async-start | bytes 4718592 | tf_op jit(solution)/shard_map/all_to_all | solution.py:423
  92.1 1.2 copy-start.1
  93.3 7.5 %copy-start.13 = (f32[384]{0:T(512)S(1)}, f32[384]{0:T(512)}, u32[]{:S(2)}) copy-start(f32[384]{0:T(512)} %constant.141.clone) | copy-start | bytes 4612
  93.3 7.7 %copy-start.10 = (bf16[768,768]{1,0:T(8,128)(2,1)S(1)}, bf16[768,768]{1,0:T(8,128)(2,1)}, u32[]{:S(2)}) copy-start(bf16[768,768]{1,0:T(8,128)(2,1)} %constant.140.clone.table_ref) | copy-start | bytes 3538948
  93.3 27.4 %all-to-all-start.1 = ((bf16[32,192,128]{2,1,0:T(8,128)(2,1)}), bf16[32,192,128]{2,1,0:T(8,128)(2,1)S(1)}, u32[]{:S(2)}, u32[]{:S(2)}) async-start(bf16[32,192,128]{2,1,0:T(8,128)(2,1)} %copy-done.1), calls=%async_computation.1 | async-start | bytes 3145728 | tf_op jit(solution)/shard_map/all_to_all | solution.py:423
  101.0 1.7 copy-start.8
  109.6 1.4 copy-start.6
  111.0 16.8 %copy-start.12 = (bf16[3,2,64,128]{3,2,1,0:T(8,128)(2,1)S(1)}, bf16[3,2,64,128]{3,2,1,0:T(8,128)(2,1)}, u32[]{:S(2)}) copy-start(bf16[3,2,64,128]{3,2,1,0:T(8,128)(2,1)} %param.10) | copy-start | bytes 294916
  120.7 106.5 %all-to-all-start.4 = ((bf16[32,288,128]{2,1,0:T(8,128)(2,1)}), bf16[32,288,128]{2,1,0:T(8,128)(2,1)}, u32[]{:S(2)}, u32[]{:S(2)}) async-start(bf16[32,288,128]{2,1,0:T(8,128)(2,1)} %copy-done.6), calls=%async_computation.4 | async-start | bytes 4718592 | tf_op jit(solution)/shard_map/all_to_all | solution.py:423
  227.2 26.3 %all-to-all-start.2 = ((bf16[32,192,128]{2,1,0:T(8,128)(2,1)}), bf16[32,192,128]{2,1,0:T(8,128)(2,1)S(1)}, u32[]{:S(2)}, u32[]{:S(2)}) async-start(bf16[32,192,128]{2,1,0:T(8,128)(2,1)} %mix.1), calls=%async_computation.2 | async-start | bytes 3145728 | tf_op jit(solution)/shard_map/all_to_all | solution.py:423
  253.5 1.1 copy-start.3
  254.7 27.9 %all-to-all-start.5 = ((bf16[32,192,128]{2,1,0:T(8,128)(2,1)}), bf16[32,192,128]{2,1,0:T(8,128)(2,1)S(1)}, u32[]{:S(2)}, u32[]{:S(2)}) async-start(bf16[32,192,128]{2,1,0:T(8,128)(2,1)} %analyse_field.1), calls=%async_computation.5 | async-start | bytes 3145728 | tf_op jit(solution)/shard_map/all_to_all | solution.py:423
  262.8 1.4 copy-start.4
  269.2 1.4 copy-start
  282.6 77.9 %all-to-all-start.3 = ((bf16[32,288,128]{2,1,0:T(8,128)(2,1)}), bf16[32,288,128]{2,1,0:T(8,128)(2,1)}, u32[]{:S(2)}, u32[]{:S(2)}) async-start(bf16[32,288,128]{2,1,0:T(8,128)(2,1)} %copy-done), calls=%async_computation.3 | async-start | bytes 4718592 | tf_op jit(solution)/shard_map/all_to_all | solution.py:423
  291.1 76.0 %reduce-scatter.2.cloned.1.call-start = ((), (), s32[]{:S(2)}) async-start(), calls=%async_computation.7 | async-start | bytes 1769472 | tf_op jit(solution)/shard_map/reduce_scatter | solution.py:460
  297.4 1.2 copy-start.2
  298.6 61.8 %copy-start.11 = (bf16[768,768]{1,0:T(8,128)(2,1)S(1)}, bf16[768,768]{1,0:T(8,128)(2,1)}, u32[]{:S(2)}) copy-start(bf16[768,768]{1,0:T(8,128)(2,1)} %constant.140.clone.table_ref) | copy-start | bytes 3538948
Sparse Core Ops, SparseCore 0:
  298.7 63.8 reduce-scatter.1

commit v2 on v1

--- a/solution.py
+++ b/solution.py
@@ -21,7 +21,6 @@
 F32 = jnp.float32
 BF16 = jnp.bfloat16
 ORDER_AXES = ("zh", "y", "lon")
-DEGREE_AXES = ("y", "dp")
 
 
 def order_of(owner, slot):
@@ -61,8 +60,34 @@
     return lax.broadcasted_iota(jnp.int32, shape, len(shape) - 1) < 64
 
 
-def dft_kernel(x_ref, table_ref, scale_ref, out_ref, held):
-    step = pl.program_id(0)
+def widen(src_ref, held, rows):
+    def body(o, _):
+        start = pl.multiple_of(o * rows, rows)
+        held[pl.ds(start, rows), :] = src_ref[o].astype(F32)
+        return 0
+
+    lax.fori_loop(0, OWNERS, body, 0)
+
+
+def narrow(held, out_ref, rows):
+    def body(o, _):
+        start = pl.multiple_of(o * rows, rows)
+        out_ref[o] = held[pl.ds(start, rows), :].astype(BF16)
+        return 0
+
+    lax.fori_loop(0, OWNERS, body, 0)
+
+
+def position():
+    z = lax.axis_index("zh") * 2 + lax.axis_index("lon")
+    return z, lax.axis_index("y"), lax.axis_index("dp")
+
+
+def place(z, y, dp):
+    return (z // 2, y, lax.rem(z, 2), dp)
+
+
+def transform(step, x_ref, table_ref, scale_ref, out_ref, held):
     x = x_ref[...].reshape(128, NLON)
     spec = lax.dot_general(
         table_ref[...], x, (((1,), (1,)), ((), ())), preferred_element_type=F32
@@ -77,32 +102,108 @@
 
     @pl.when(step == JD // 2 - 1)
     def _():
-        def body(o, _):
-            start = pl.multiple_of(o * 288, 288)
-            out_ref[o] = held[pl.ds(start, 288), :].astype(BF16)
-            return 0
-
-        lax.fori_loop(0, OWNERS, body, 0)
+        narrow(held, out_ref, 288)
+
+
+def dft_kernel(x_ref, table_ref, scale_ref, out_ref, held):
+    transform(pl.program_id(0), x_ref, table_ref, scale_ref, out_ref, held)
+
+
+def dft_gather_kernel(
+    x_ref, table_ref, scale_ref, weight_ref, out_ref, gathered_ref, held, sent, got, own
+):
+    step = pl.program_id(0)
+    z, y, dp = position()
+
+    def copy(t):
+        peer = lax.rem(z + t, 8)
+        return pltpu.make_async_remote_copy(
+            src_ref=weight_ref,
+            dst_ref=gathered_ref.at[z],
+            send_sem=sent.at[t],
+            recv_sem=got.at[t],
+            device_id=place(peer, y, dp),
+            device_id_type=pl.DeviceIdType.MESH,
+        )
+
+    def keep():
+        return pltpu.make_async_copy(weight_ref, gathered_ref.at[z], own)
+
+    @pl.when(step == 0)
+    def _():
+        barrier = pltpu.get_barrier_semaphore()
+        for t in range(1, 8):
+            pl.semaphore_signal(
+                barrier,
+                inc=1,
+                device_id=place(lax.rem(z + t, 8), y, dp),
+                device_id_type=pl.DeviceIdType.MESH,
+            )
+        pl.semaphore_wait(barrier, 7)
+        for t in range(1, 8):
+            copy(t).start()
+        keep().start()
+
+    transform(step, x_ref, table_ref, scale_ref, out_ref, held)
+
+    @pl.when(step == JD // 2 - 1)
+    def _():
+        for t in range(1, 8):
+            copy(t).wait()
+        keep().wait()
+
+
+def dft_inputs():
+    return [
+        pl.BlockSpec((2, 64, NLON), lambda s: (s, 0, 0)),
+        pl.BlockSpec((2 * L, NLON), lambda s: (0, 0)),
+        pl.BlockSpec((2, 1, 128), lambda s: (s, 0, 0)),
+    ]
+
+
+def dft_cost():
+    return pl.CostEstimate(flops=2 * 1536 * 768 * 768, bytes_accessed=6_000_000, transcendentals=0)
 
 
 def dft(x, table, scale):
     return pl.pallas_call(
         dft_kernel,
         grid=(JD // 2,),
-        in_specs=[
-            pl.BlockSpec((2, 64, NLON), lambda s: (s, 0, 0)),
-            pl.BlockSpec((2 * L, NLON), lambda s: (0, 0)),
-            pl.BlockSpec((2, 1, 128), lambda s: (s, 0, 0)),
-        ],
+        in_specs=dft_inputs(),
         out_specs=pl.BlockSpec((OWNERS, 288, 128), lambda s: (0, 0, 0)),
         out_shape=jax.ShapeDtypeStruct((OWNERS, 288, 128), BF16),
         scratch_shapes=[pltpu.VMEM((L * JD, 128), F32)],
         compiler_params=params(40),
-        cost_estimate=pl.CostEstimate(
-            flops=2 * 1536 * 768 * 768, bytes_accessed=6_000_000, transcendentals=0
-        ),
+        cost_estimate=dft_cost(),
         name="dft",
     )(x, table, scale)
+
+
+def dft_gather(x, table, scale, weight):
+    return pl.pallas_call(
+        dft_gather_kernel,
+        grid=(JD // 2,),
+        in_specs=dft_inputs() + [pl.BlockSpec(memory_space=pl.ANY)],
+        out_specs=[
+            pl.BlockSpec((OWNERS, 288, 128), lambda s: (0, 0, 0)),
+            pl.BlockSpec(memory_space=pl.ANY),
+        ],
+        out_shape=[
+            jax.ShapeDtypeStruct((OWNERS, 288, 128), BF16),
+            jax.ShapeDtypeStruct((8, L, 128), BF16),
+        ],
+        scratch_shapes=[
+            pltpu.VMEM((L * JD, 128), F32),
+            pltpu.SemaphoreType.DMA((8,)),
+            pltpu.SemaphoreType.DMA((8,)),
+            pltpu.SemaphoreType.DMA,
+        ],
+        compiler_params=pltpu.CompilerParams(
+            vmem_limit_bytes=40 * MIB, collective_id=1, has_side_effects=True
+        ),
+        cost_estimate=dft_cost(),
+        name="dft_gather",
+    )(x, table, scale, weight)
 
 
 def legendre_kernel(order_ref, seed_ref, unscale_ref, cos_ref, up_ref, down_ref, out_ref, held):
@@ -196,27 +297,8 @@
     )
 
 
-def widen(src_ref, held, rows):
-    def body(o, _):
-        start = pl.multiple_of(o * rows, rows)
-        held[pl.ds(start, rows), :] = src_ref[o].astype(F32)
-        return 0
-
-    lax.fori_loop(0, OWNERS, body, 0)
-
-
-def narrow(held, out_ref, rows):
-    def body(o, _):
-        start = pl.multiple_of(o * rows, rows)
-        out_ref[o] = held[pl.ds(start, rows), :].astype(BF16)
-        return 0
-
-    lax.fori_loop(0, OWNERS, body, 0)
-
-
-def analyse_kernel(spec_ref, table_ref, factor_ref, out_ref, field, packed):
+def analyse(spec_ref, table_ref, factor_ref, out_ref, field, packed):
     widen(spec_ref, field, 288)
-    packed[...] = jnp.zeros_like(packed)
     for k in range(SLOTS):
         first = k // 3
         columns = []
@@ -228,7 +310,9 @@
             columns.append(jnp.concatenate(pieces, axis=0).astype(BF16))
         data = jnp.concatenate(columns, axis=1)
         rows = table_ref[k * L + 96 * first : (k + 1) * L, :]
-        result = jnp.dot(rows, data, preferred_element_type=F32) * factor_ref[k : k + 1, :]
+        result = jnp.dot(rows, data, preferred_element_type=F32)
+        if factor_ref is not None:
+            result = result * factor_ref[k : k + 1, :]
         for group in range(first, 4):
             for i in range(3):
                 at = ((group - first) * 3 + i) * 32
@@ -240,21 +324,6 @@
     narrow(packed, out_ref, 192)
 
 
-def analyse(spec, table, factor, name):
-    return pl.pallas_call(
-        analyse_kernel,
-        in_specs=[vmem_spec()] * 3,
-        out_specs=vmem_spec(),
-        out_shape=jax.ShapeDtypeStruct((OWNERS, 192, 128), BF16),
-        scratch_shapes=[pltpu.VMEM((OWNERS * 288, 128), F32), pltpu.VMEM((OWNERS * 192, 128), F32)],
-        compiler_params=params(48),
-        cost_estimate=pl.CostEstimate(
-            flops=2 * 12 * 384 * 384 * 256, bytes_accessed=8_000_000, transcendentals=0
-        ),
-        name=name,
-    )(spec, table, factor)
-
-
 def degree_rows(held, group, i):
     parts = []
     for lon in range(2):
@@ -266,9 +335,8 @@
     return jnp.concatenate(parts, axis=1)
 
 
-def mix_kernel(grad_ref, weight_ref, out_ref, held, packed):
+def mix(grad_ref, weight_ref, out_ref, held, packed):
     widen(grad_ref, held, 192)
-    packed[...] = jnp.zeros_like(packed)
     for group in range(4):
         for i in range(3):
             rows = degree_rows(held, group, i)
@@ -287,22 +355,7 @@
     narrow(packed, out_ref, 192)
 
 
-def mix(grads, weights):
-    return pl.pallas_call(
-        mix_kernel,
-        in_specs=[vmem_spec()] * 2,
-        out_specs=vmem_spec(),
-        out_shape=jax.ShapeDtypeStruct((OWNERS, 192, 128), BF16),
-        scratch_shapes=[pltpu.VMEM((OWNERS * 192, 128), F32)] * 2,
-        compiler_params=params(40),
-        cost_estimate=pl.CostEstimate(
-            flops=2 * 2880 * 256 * 256, bytes_accessed=5_000_000, transcendentals=0
-        ),
-        name="mix",
-    )(grads, weights)
-
-
-def weight_grad_kernel(coeff_ref, grad_ref, out_ref, held_c, held_g):
+def weight_grads(coeff_ref, grad_ref, out_ref, held_c, held_g):
     widen(coeff_ref, held_c, 192)
     widen(grad_ref, held_g, 192)
     low = low_half((64, 128))
@@ -323,28 +376,13 @@
                 first, second = turned
                 out_ref[2 * group + lon, 128 * i : 128 * i + 64, :] = jnp.where(
                     low, first, pltpu.roll(second, 64, 1)
-                )
+                ).astype(out_ref.dtype)
                 out_ref[2 * group + lon, 128 * i + 64 : 128 * i + 128, :] = jnp.where(
                     low, pltpu.roll(first, 64, 1), second
-                )
-
-
-def weight_grads(coeffs, grads):
-    return pl.pallas_call(
-        weight_grad_kernel,
-        in_specs=[vmem_spec()] * 2,
-        out_specs=vmem_spec(),
-        out_shape=jax.ShapeDtypeStruct((8, 384, 128), F32),
-        scratch_shapes=[pltpu.VMEM((OWNERS * 192, 128), F32)] * 2,
-        compiler_params=params(40),
-        cost_estimate=pl.CostEstimate(
-            flops=2 * 2880 * 256 * 256, bytes_accessed=5_000_000, transcendentals=0
-        ),
-        name="weight_grads",
-    )(coeffs, grads)
-
-
-def synthesise_kernel(mixed_ref, table_ref, quad_ref, out_ref, held, grid):
+                ).astype(out_ref.dtype)
+
+
+def synthesise(mixed_ref, table_ref, quad_ref, out_ref, held, grid):
     widen(mixed_ref, held, 192)
     for k in range(SLOTS):
         first = k // 3
@@ -369,19 +407,172 @@
     narrow(grid, out_ref, 288)
 
 
-def synthesise(mixed, table, quad):
+def core_kernel(
+    spec_ref,
+    field_ref,
+    table_ref,
+    weight_ref,
+    factor_ref,
+    quad_ref,
+    grid_ref,
+    partial_ref,
+    field_in,
+    grid_out,
+    degree_out,
+    degree_in,
+    partial_out,
+    wide,
+    packed_a,
+    packed_b,
+    order_sent,
+    order_got,
+    degree_sent,
+    degree_got,
+    z_sent,
+    z_got,
+):
+    z, y, dp = position()
+    me_order = ((z // 2) * 4 + y) * 2 + lax.rem(z, 2)
+    me_degree = y * 8 + dp
+
+    def order_peer(t):
+        at = lax.rem(t * 13, 32)
+        return lax.rem(z + lax.rem(at, 8), 8), lax.rem(y + at // 8, 4)
+
+    def degree_peer(t):
+        at = lax.rem(t * 13, 32)
+        return lax.rem(y + lax.rem(at, 4), 4), lax.rem(dp + at // 4, 8)
+
+    def order_copy(n, src, dst, t):
+        pz, py = order_peer(t)
+        return pltpu.make_async_remote_copy(
+            src_ref=src.at[((pz // 2) * 4 + py) * 2 + lax.rem(pz, 2)],
+            dst_ref=dst.at[me_order],
+            send_sem=order_sent.at[n, t],
+            recv_sem=order_got.at[n, t],
+            device_id=place(pz, py, dp),
+            device_id_type=pl.DeviceIdType.MESH,
+        )
+
+    def degree_copy(n, t):
+        py, pd = degree_peer(t)
+        return pltpu.make_async_remote_copy(
+            src_ref=degree_out.at[n, py * 8 + pd],
+            dst_ref=degree_in.at[n, me_degree],
+            send_sem=degree_sent.at[n, t],
+            recv_sem=degree_got.at[n, t],
+            device_id=place(z, py, pd),
+            device_id_type=pl.DeviceIdType.MESH,
+        )
+
+    def z_copy(t):
+        pz = lax.rem(z + t, 8)
+        return pltpu.make_async_remote_copy(
+            src_ref=partial_out.at[pz],
+            dst_ref=partial_ref.at[z],
+            send_sem=z_sent.at[t],
+            recv_sem=z_got.at[t],
+            device_id=place(pz, y, dp),
+            device_id_type=pl.DeviceIdType.MESH,
+        )
+
+    def each(first, end, action):
+        def body(t, _):
+            action(t)
+            return 0
+
+        lax.fori_loop(first, end, body, 0)
+
+    def send_field(first, end):
+        each(first, end, lambda t: order_copy(0, field_ref, field_in, t).start())
+
+    def send_grid(first, end):
+        each(first, end, lambda t: order_copy(1, grid_out, grid_ref, t).start())
+
+    def send_degrees(n):
+        each(1, 32, lambda t: degree_copy(n, t).start())
+        degree_in[n, me_degree] = degree_out[n, me_degree]
+
+    def wait_degrees(n):
+        each(1, 32, lambda t: degree_copy(n, t).wait())
+
+    barrier = pltpu.get_barrier_semaphore()
+
+    def greet(t):
+        pz, py = order_peer(t)
+        pl.semaphore_signal(
+            barrier, inc=1, device_id=place(pz, py, dp), device_id_type=pl.DeviceIdType.MESH
+        )
+        py, pd = degree_peer(t)
+        pl.semaphore_signal(
+            barrier, inc=1, device_id=place(z, py, pd), device_id_type=pl.DeviceIdType.MESH
+        )
+
+    each(1, 32, greet)
+    pl.semaphore_wait(barrier, 62)
+
+    send_field(1, 9)
+    field_in[me_order] = field_ref[me_order]
+    packed_a[...] = jnp.zeros_like(packed_a)
+    packed_b[...] = jnp.zeros_like(packed_b)
+    analyse(spec_ref, table_ref, factor_ref, degree_out.at[0], wide, packed_a)
+    send_degrees(0)
+    send_field(9, 21)
+    wait_degrees(0)
+    mix(degree_in.at[0], weight_ref, degree_out.at[1], packed_b, packed_a)
+    send_degrees(1)
+    send_field(21, 32)
+    wait_degrees(1)
+    synthesise(degree_in.at[1], table_ref, quad_ref, grid_out, packed_b, wide)
+    send_grid(1, 9)
+    grid_ref[me_order] = grid_out[me_order]
+    each(1, 32, lambda t: order_copy(0, field_ref, field_in, t).wait())
+    analyse(field_in, table_ref, None, degree_out.at[2], wide, packed_a)
+    send_degrees(2)
+    send_grid(9, 20)
+    wait_degrees(2)
+    send_grid(20, 24)
+    weight_grads(degree_in.at[2], degree_in.at[0], partial_out, packed_a, packed_b)
+    each(1, 8, lambda t: z_copy(t).start())
+    partial_ref[z] = partial_out[z]
+    send_grid(24, 32)
+    each(1, 8, lambda t: z_copy(t).wait())
+    each(1, 32, lambda t: order_copy(1, grid_out, grid_ref, t).wait())
+
+
+def core(spec, field, table, weights, factor, quad):
     return pl.pallas_call(
-        synthesise_kernel,
-        in_specs=[vmem_spec()] * 3,
-        out_specs=vmem_spec(),
-        out_shape=jax.ShapeDtypeStruct((OWNERS, 288, 128), BF16),
-        scratch_shapes=[pltpu.VMEM((OWNERS * 192, 128), F32), pltpu.VMEM((OWNERS * 288, 128), F32)],
-        compiler_params=params(48),
+        core_kernel,
+        in_specs=[vmem_spec()] * 6,
+        out_specs=[vmem_spec()] * 2,
+        out_shape=[
+            jax.ShapeDtypeStruct((OWNERS, 288, 128), BF16),
+            jax.ShapeDtypeStruct((8, L, 128), BF16),
+        ],
+        scratch_shapes=[
+            pltpu.VMEM((OWNERS, 288, 128), BF16),
+            pltpu.VMEM((OWNERS, 288, 128), BF16),
+            pltpu.VMEM((3, OWNERS, 192, 128), BF16),
+            pltpu.VMEM((3, OWNERS, 192, 128), BF16),
+            pltpu.VMEM((8, L, 128), BF16),
+            pltpu.VMEM((OWNERS * 288, 128), F32),
+            pltpu.VMEM((OWNERS * 192, 128), F32),
+            pltpu.VMEM((OWNERS * 192, 128), F32),
+            pltpu.SemaphoreType.DMA((2, 32)),
+            pltpu.SemaphoreType.DMA((2, 32)),
+            pltpu.SemaphoreType.DMA((3, 32)),
+            pltpu.SemaphoreType.DMA((3, 32)),
+            pltpu.SemaphoreType.DMA((8,)),
+            pltpu.SemaphoreType.DMA((8,)),
+        ],
+        compiler_params=pltpu.CompilerParams(
+            vmem_limit_bytes=58 * MIB, collective_id=2, has_side_effects=True
+        ),
         cost_estimate=pl.CostEstimate(
-            flops=2 * 12 * 384 * 384 * 256, bytes_accessed=8_000_000, transcendentals=0
+            flops=7_000_000_000, bytes_accessed=16_000_000, transcendentals=0
         ),
-        name="synthesise",
-    )(mixed, table, quad)
+        name="core",
+    )(spec, field, table, weights, factor, quad)
 
 
 def inverse_kernel(spec_ref, table_ref, out_ref, held, turned):
@@ -441,23 +632,18 @@
     quad = jnp.asarray(np.broadcast_to(quad[:, None], (NLAT, 128)))
     local_quad = lax.dynamic_slice_in_dim(quad, lat_rank * JD, JD, 0).reshape(JD, 1, 128)
 
-    spec_out = exchange(dft(cotangent[0], table, jnp.ones((JD, 1, 128), F32)), ORDER_AXES)
-    spec_in = exchange(dft(inputs[0], table, local_quad), ORDER_AXES)
-    gathered = lax.all_gather(weight, ("zh", "lon"), axis=0, tiled=False)
+    spec_out, gathered = dft_gather(
+        cotangent[0], table, jnp.ones((JD, 1, 128), F32), weight.reshape(L, 128)
+    )
+    spec_out = exchange(spec_out, ORDER_AXES)
+    spec_in = dft(inputs[0], table, local_quad)
     weights = mixing_matrices(gathered)
     legend = legendre(owner)
-
     base = 1.0 / math.sqrt(NLAT)
     factor = jnp.full((16, 256), 2.0 * base, F32)
     factor = factor.at[0].set(jnp.where(owner == 0, base, 2.0 * base))
-    grads = exchange(analyse(spec_out, legend, factor, "analyse_grad"), DEGREE_AXES)
-    mixed = exchange(mix(grads, weights), DEGREE_AXES)
-    grid = exchange(synthesise(mixed, legend, quad), ORDER_AXES)
-    coeffs = exchange(
-        analyse(spec_in, legend, jnp.ones((16, 256), F32), "analyse_field"), DEGREE_AXES
-    )
-    partial = weight_grads(coeffs, grads)
-    weight_grad = lax.psum_scatter(partial, ("zh", "lon"), scatter_dimension=0, tiled=False)
+    grid, partial = core(spec_out, spec_in, legend, weights, factor, quad)
+    weight_grad = jnp.sum(partial.astype(F32), axis=0)
     field = inverse(grid, table)
     return field[None], weight_grad.reshape(3, 2, 64, 128)
 

time: 378 us -> 268 us (0.71)
  Pallas kernels: 66.1 us -> 217 us
  waiting for transfers between devices: 133 us -> 15.9 us
  blocking collectives: 76.1 us -> 0 us
  starting transfers between devices: 49.5 us -> 8.64 us
  between operations: 14.4 us -> 0.87 us
  local copies, waits for them, and re-layouts: 33.3 us -> 20.6 us
    pallas_call x7 -> x3, Pallas kernels: 44.1 us -> 197 us  [the longest x1 163 us: core(): pl.pallas_call(core_kernel, in_specs=[vmem_spec()] * 6, out_specs=[vmem_s...]
    all_to_all x6 -> x1, waiting for transfers between devices: 133 us -> 15.9 us  [exchange(): return lax.all_to_all(x, axes, split_axis=0, concat_axis=0, tiled=True)]
    all_gather x1 -> x0, blocking collectives: 76.1 us -> none  [shards(): gathered = lax.all_gather(weight, ('zh', 'lon'), axis=0, tiled=False)]
    all_to_all x6 -> x1, starting transfers between devices: 49.5 us -> 8.64 us  [exchange(): return lax.all_to_all(x, axes, split_axis=0, concat_axis=0, tiled=True)]
    unnamed x30 -> x20, local copies, waits for them, and re-layouts: 13.7 us -> 6.91 us
  transfers between devices with their start and end apart: 7 -> 1, of which waited for: 5 -> 1; matrix products, arithmetic and copies ran while one was open for 6% -> 5% of each run, Pallas kernels for 14% -> 8%
where the time goes in v2:
time: 268 us; the launch traced here: 266 us
  Pallas kernels  217 us (81%)
  local copies, waits for them, and re-layouts  20.6 us (8%)
  waiting for transfers between devices  15.9 us (6%)
  starting transfers between devices  8.64 us (3%)
  other arithmetic  2.78 us (1%)
    pallas_call x1, Pallas kernels, core(): pl.pallas_call(core_kernel, in_specs=[vmem_spec()] * 6, out_specs=[vmem_s...  163 us
    pallas_call x1, Pallas kernels, dft_gather(): pl.pallas_call(dft_gather_kernel, grid=(JD // 2,), in_specs=dft_inputs()...  27.1 us
    all_to_all x1, waiting for transfers between devices, exchange(): return lax.all_to_all(x, axes, split_axis=0, concat_axis=0, tiled=True)  15.9 us
    pallas_call x1, Pallas kernels, legendre(): pl.pallas_call(legendre_kernel, in_specs=[vmem_spec()] * 6, out_specs=vme...  15.3 us
    all_to_all x1, starting transfers between devices, exchange(): return lax.all_to_all(x, axes, split_axis=0, concat_axis=0, tiled=True)  8.64 us
    pallas_call x1, Pallas kernels, dft(): pl.pallas_call(dft_kernel, grid=(JD // 2,), in_specs=dft_inputs(), out_sp...  6.92 us
    unnamed x20, local copies, waits for them, and re-layouts  6.91 us
  transfers between devices with their start and end apart: 1, of which 1 were waited for; matrix products, arithmetic and copies ran while one was open for 5% of the time, Pallas kernels for 8%

profile of v2, /device:TPU:18, one launch (start us, length us, event | category | flops | bytes accessed | tf_op | source)
XLA Modules:
  0.0 266.1 jit_solution(6585848538345621298)
XLA Ops:
  0.6 0.0 copy-start
  0.7 1.7 copy-done
  2.3 0.0 copy-start.2
  2.3 0.9 copy-done.2
  3.2 0.0 copy-start.3
  3.2 1.3 copy-done.3
  4.5 27.1 %dft_gather.1 = (bf16[32,288,128]{2,1,0:T(8,128)(2,1)}, bf16[8,384,128]{2,1,0:T(8,128)(2,1)S(1)}) custom-call(bf16[24,64,768]{2,1,0:T(8,128)(2,1)S(1)} %bitcast.18, bf16[768,768]{1,0:T(8,128)(2,1)S(1)} %copy-done.3, f32[24,1,128]{2,1,0:T(1,128)S(1)} %broadcast_in_dim.12.scale_ref, bf16[384,128]{1,0:T(8,128)(2,1)S(1)} %bitcast.20), custom_call_target="tpu_custom_call" | custom-call | flops 1811939328 | bytes 6000000 | tf_op jit(solution)/shard_map/dft_gather/pallas_call | solution.py:183
  31.5 0.0 copy-start.9
  31.6 8.6 %all-to-all-start = ((bf16[32,288,128]{2,1,0:T(8,128)(2,1)}), bf16[32,288,128]{2,1,0:T(8,128)(2,1)}, u32[]{:S(2)}, u32[]{:S(2)}) async-start(bf16[32,288,128]{2,1,0:T(8,128)(2,1)} %get-tuple-element.18), calls=%async_computation | async-start | bytes 4718592 | tf_op jit(solution)/shard_map/all_to_all | solution.py:614
  40.3 0.0 copy-done.9
  40.3 0.2 select_reduce_fusion
  40.5 0.1 divide_sqrt_fusion
  40.6 0.1 copy.14
  40.7 0.1 copy.15
  40.8 0.7 reshape.265
  41.6 1.3 fusion.10
  42.9 0.2 fusion.9
  43.1 0.4 copy_bitcast_fusion
  43.5 0.6 maximum_bitcast_fusion.1
  44.1 0.7 maximum_bitcast_fusion
  44.8 3.2 %copy.18 = bf16[4,3,2,2,64,2,2,64]{7,6,5,4,3,2,1,0:T(2,128)(2,1)S(1)} copy(bf16[4,3,2,2,64,2,2,64]{7,4,6,5,1,2,0,3:T(8,128)(2,1)S(1)} %maximum_bitcast_fusion) | data formatting | bytes 3145728 | tf_op jit(solution)/shard_map/transpose | solution.py:623
  48.0 0.0 copy-start.8
  48.1 3.0 %reshape.266.weight_ref = bf16[12,256,256]{2,1,0:T(8,128)(2,1)} reshape(bf16[4,3,2,2,64,2,2,64]{7,6,5,4,3,2,1,0:T(2,128)(2,1)S(1)} %copy.18) | data formatting | bytes 3145728 | tf_op jit(solution)/shard_map/reshape | solution.py:623
  51.1 0.0 copy-done.8
  51.1 0.1 dynamic-slice.6
  51.2 0.1 negate_exponential_fusion
  51.3 0.9 broadcast_in_dim.15.up_ref
  52.2 2.2 broadcast_in_dim.16.down_ref
  54.4 0.1 broadcast_in_dim.13.order_ref
  54.5 0.0 copy-start.1
  54.5 0.0 copy-start.4
  54.5 15.3 %legendre.1.table_ref = bf16[4608,384]{1,0:T(8,128)(2,1)} custom-call(s32[16,128]{1,0:T(8,128)S(1)} %broadcast_in_dim.13.order_ref, f32[16,384]{1,0:T(8,128)S(1)} %get-tuple-element.27.seed_ref, f32[16,384]{1,0:T(8,128)S(1)} %get-tuple-element.26.unscale_ref, f32[16,384]{1,0:T(8,128)S(1)} %broadcast_in_dim.14.cos_ref, ...), custom_call_target="tpu_custom_call" | custom-call | flops 23592960 | bytes 10000000 | tf_op jit(solution)/shard_map/legendre/pallas_call | solution.py:279
  69.8 0.1 broadcast.463.scale_ref
  69.9 0.0 copy-done.1
  69.9 0.0 copy-done.4
  69.9 6.9 %dft.1.field_ref = bf16[32,288,128]{2,1,0:T(8,128)(2,1)S(1)} custom-call(bf16[24,64,768]{2,1,0:T(8,128)(2,1)S(1)} %bitcast.19, bf16[768,768]{1,0:T(8,128)(2,1)S(1)} %copy-done.4, f32[24,1,128]{2,1,0:T(1,128)S(1)} %broadcast.463.scale_ref), custom_call_target="tpu_custom_call" | custom-call | flops 1811939328 | bytes 6000000 | tf_op jit(solution)/shard_map/dft/pallas_call | solution.py:169
  76.8 0.0 copy-start.5
  76.9 1.4 copy-done.5
  78.2 15.9 %all-to-all-done.spec_ref = bf16[32,288,128]{2,1,0:T(8,128)(2,1)} async-done(((bf16[32,288,128]{2,1,0:T(8,128)(2,1)}), bf16[32,288,128]{2,1,0:T(8,128)(2,1)}, u32[]{:S(2)}, u32[]{:S(2)}) %all-to-all-start) | async-done | bytes 2359328 | tf_op jit(solution)/shard_map/all_to_all | solution.py:614
  94.1 0.7 scatter.8.factor_ref
  94.8 0.8 jit_solution_.3.quad_ref
  95.6 163.0 %core.1 = (bf16[32,288,128]{2,1,0:T(8,128)(2,1)}, bf16[8,384,128]{2,1,0:T(8,128)(2,1)}) custom-call(bf16[32,288,128]{2,1,0:T(8,128)(2,1)} %all-to-all-done.spec_ref, bf16[32,288,128]{2,1,0:T(8,128)(2,1)} %copy-done.5, bf16[4608,384]{1,0:T(8,128)(2,1)} %legendre.1.table_ref, bf16[12,256,256]{2,1,0:T(8,128)(2,1)} %reshape.266.weight_ref, ...), custom_call_target="tpu_custom_call" | custom-call | flops 7000000000 | bytes 16000000 | tf_op jit(solution)/shard_map/core/pallas_call | solution.py:544
  258.6 0.0 copy-start.6
  258.6 1.7 copy-done.6
  260.2 0.0 copy-start.7
  260.2 5.1 %inverse_dft.1 = bf16[24,64,768]{2,1,0:T(8,128)(2,1)} custom-call(bf16[32,288,128]{2,1,0:T(8,128)(2,1)S(1)} %copy-done.6, bf16[768,768]{1,0:T(8,128)(2,1)S(1)} %copy-done.4), custom_call_target="tpu_custom_call" | custom-call | flops 1811939328 | bytes 6000000 | tf_op jit(solution)/shard_map/inverse_dft/pallas_call | solution.py:595
  265.3 0.0 copy-done.7
  265.3 0.8 convert_reduce_fusion
  (10 shorter events, 0.2 us)
Async XLA Ops:
  0.6 1.7 copy-start
  2.3 0.9 copy-start.2
  3.2 1.3 copy-start.3
  31.5 8.7 %copy-start.9 = (f32[384]{0:T(512)S(1)}, f32[384]{0:T(512)}, u32[]{:S(2)}) copy-start(f32[384]{0:T(512)} %constant.147) | copy-start | bytes 4612
  31.6 62.6 %all-to-all-start = ((bf16[32,288,128]{2,1,0:T(8,128)(2,1)}), bf16[32,288,128]{2,1,0:T(8,128)(2,1)}, u32[]{:S(2)}, u32[]{:S(2)}) async-start(bf16[32,288,128]{2,1,0:T(8,128)(2,1)} %get-tuple-element.18), calls=%async_computation | async-start | bytes 4718592 | tf_op jit(solution)/shard_map/all_to_all | solution.py:614
  48.0 3.0 %copy-start.8 = (f32[384]{0:T(512)S(1)}, f32[384]{0:T(512)}, u32[]{:S(2)}) copy-start(f32[384]{0:T(512)} %constant.140.clone) | copy-start | bytes 4612
  54.5 15.4 %copy-start.1 = (bf16[1,24,64,768]{3,2,1,0:T(8,128)(2,1)S(1)}, bf16[1,24,64,768]{3,2,1,0:T(8,128)(2,1)}, u32[]{:S(2)}) copy-start(bf16[1,24,64,768]{3,2,1,0:T(8,128)(2,1)} %param.8) | copy-start | bytes 7077892
  54.5 15.4 %copy-start.4 = (bf16[768,768]{1,0:T(8,128)(2,1)S(1)}, bf16[768,768]{1,0:T(8,128)(2,1)}, u32[]{:S(2)}) copy-start(bf16[768,768]{1,0:T(8,128)(2,1)} %constant.139.clone.table_ref) | copy-start | bytes 3538948
  76.8 1.4 copy-start.5
  258.6 1.7 copy-start.6
  260.2 5.1 %copy-start.7 = (bf16[8,384,128]{2,1,0:T(8,128)(2,1)S(1)}, bf16[8,384,128]{2,1,0:T(8,128)(2,1)}, u32[]{:S(2)}) copy-start(bf16[8,384,128]{2,1,0:T(8,128)(2,1)} %get-tuple-element.21) | copy-start | bytes 2359300

commit v3 on v1

v3 whole, which is shorter than its diff:
```python
import math

import jax
import jax.numpy as jnp
import numpy as np
from jax import lax
from jax.experimental import pallas as pl
from jax.experimental.pallas import tpu as pltpu
from jax.sharding import Mesh
from jax.sharding import PartitionSpec as P

L = 384
NLON = 768
NLAT = 384
C = 128
OWNERS = 32
SLOTS = 12
JD = 24
MIB = 1024 * 1024
F32 = jnp.float32
BF16 = jnp.bfloat16


def order_of(owner, slot):
    half = slot // 2
    return 64 * half + owner if slot % 2 == 0 else 64 * half + 63 - owner


SETS = (range(0, 4), range(4, SLOTS))
SET_ROWS = 96
HALF_ROWS = 48
ALL_ROWS = 192


def row_index():
    table = {}
    for number, slots in enumerate(SETS):
        count = 0
        for slot in slots:
            for group in range(slot // 3, 4):
                for i in range(3):
                    for lon in range(2):
                        table[slot, group, i, lon] = SET_ROWS * number + HALF_ROWS * lon + count
                    count += 1
    return table


ROWS = row_index()


def fourier_rows():
    orders = np.array([order_of(o, k) for o in range(OWNERS) for k in range(SLOTS)], np.int64)
    phase = (orders[:, None] * np.arange(NLON)[None, :] % NLON) * (2.0 * math.pi / NLON)
    rows = np.concatenate([np.cos(phase), -np.sin(phase)], axis=0) / math.sqrt(NLON)
    return rows.astype(np.float32).astype(jnp.bfloat16)


def legendre_seeds():
    lat = np.arange(NLAT, dtype=np.float64)
    sine = np.sin(math.pi * (lat + 0.5) / NLAT)
    steps = np.arange(1, L, dtype=np.float64)
    cumlog = np.concatenate([np.zeros(1), np.cumsum(np.log1p(-0.5 / steps))])
    orders = np.array(
        [[min(order_of(o, k), L - 1) for k in range(16)] for o in range(OWNERS)], np.int64
    )
    m = orders[:, :, None].astype(np.float64)
    log_start = 0.5 * (
        np.log(2.0 * m + 1.0) - math.log(4.0 * math.pi) + cumlog[orders][:, :, None]
    ) + m * np.log(sine)[None, None, :]
    shift = np.clip(-log_start - 60.0, 0.0, 80.0)
    seed = np.exp(log_start + shift)
    seed = np.where(seed < 1.2e-38, 0.0, seed)
    return seed.astype(np.float32), np.exp(-shift).astype(np.float32)


def low_half(shape):
    return lax.broadcasted_iota(jnp.int32, shape, len(shape) - 1) < 64


def position():
    z = lax.axis_index("zh") * 2 + lax.axis_index("lon")
    return z, lax.axis_index("y"), lax.axis_index("dp")


def place(z, y, dp):
    return (z // 2, y, lax.rem(z, 2), dp)


def widen(src_ref, held, stride, first, rows):
    def body(o, _):
        start = pl.multiple_of(o * stride + first, 16)
        held[pl.ds(start, rows), :] = src_ref[o, first : first + rows, :].astype(F32)
        return 0

    lax.fori_loop(0, OWNERS, body, 0)


def narrow(held, out_ref, stride, first, rows):
    def body(o, _):
        start = pl.multiple_of(o * stride + first, 16)
        out_ref[o, first : first + rows, :] = held[pl.ds(start, rows), :].astype(BF16)
        return 0

    lax.fori_loop(0, OWNERS, body, 0)


def transform(x_ref, fourier_ref, out_ref, held, scale_of):
    low = low_half((L, 128))

    def body(step, _):
        x = x_ref[pl.ds(2 * step, 2)].reshape(128, NLON)
        spec = lax.dot_general(
            fourier_ref[...], x, (((1,), (1,)), ((), ())), preferred_element_type=F32
        )
        real, imag = spec[:L], spec[L:]
        even = jnp.where(low, real, pltpu.roll(imag, 64, 1))
        odd = jnp.where(low, pltpu.roll(real, 64, 1), imag)
        if scale_of is not None:
            even = even * scale_of(2 * step)
            odd = odd * scale_of(2 * step + 1)
        held[pl.ds(2 * step, L, stride=JD), :] = even
        held[pl.ds(2 * step + 1, L, stride=JD), :] = odd
        return 0

    lax.fori_loop(0, JD // 2, body, 0)
    narrow(held, out_ref, 288, 0, 288)


def legendre(owner, seed_ref, unscale_ref, cos_ref, out_ref, pool):
    slot = lax.broadcasted_iota(jnp.int32, (16, 128), 0)
    half = 64 * (slot // 2)
    order = jnp.where(lax.rem(slot, 2) == 0, half + owner, half + 63 - owner)
    order = jnp.minimum(order, L - 1)
    order_f = order.astype(F32)
    square = order_f * order_f
    cosine = cos_ref[...]

    def advance(degree, row, previous, before):
        degree_f = jnp.full((16, 128), degree, jnp.int32).astype(F32)
        up = jnp.sqrt(
            jnp.maximum(4.0 * degree_f * degree_f - 1.0, 1.0)
            / jnp.maximum(degree_f * degree_f - square, 1.0)
        )
        lower = degree_f - 1.0
        down = jnp.sqrt(
            jnp.maximum(lower * lower - square, 0.0)
            / jnp.maximum(4.0 * lower * lower - 1.0, 1.0)
        )
        fresh = []
        for c in range(3):
            lanes = slice(128 * c, 128 * c + 128)
            value = up * (cosine[:, lanes] * previous[c] - down * before[c])
            value = jnp.where(order == degree, seed_ref[:, lanes], value)
            value = jnp.where(order > degree, 0.0, value)
            pool[pl.ds(16 * L * c + row, 16, stride=L), :] = value * unscale_ref[:, lanes]
            fresh.append(value)
        return fresh, previous

    def body(step, carry):
        previous, before = list(carry[:3]), list(carry[3:])
        group = step // 32
        d = step - 32 * group
        for i in range(3):
            previous, before = advance(3 * step + i, 96 * group + 32 * i + d, previous, before)
        return tuple(previous) + tuple(before)

    zero = jnp.zeros((16, 128), F32)
    lax.fori_loop(0, L // 3, body, (zero,) * 6)

    def convert(k, _):
        start = pl.multiple_of(k * L, L)
        for c in range(3):
            out_ref[pl.ds(start, L), 128 * c : 128 * c + 128] = pool[
                pl.ds(16 * L * c + start, L), :
            ].astype(BF16)
        return 0

    lax.fori_loop(0, SLOTS, convert, 0)


def mixing_matrices(gathered_ref, out_ref):
    low = low_half((64, 128))
    for group in range(4):
        for i in range(3):
            for lon in range(2):
                source = gathered_ref[2 * group + lon, 128 * i : 128 * i + 128, :].astype(F32)
                real, imag = source[:64], source[64:]
                real_t, imag_t = pltpu.roll(real, 64, 1), pltpu.roll(imag, 64, 1)
                n, at = group * 3 + i, 128 * lon
                out_ref[n, at : at + 64, :128] = jnp.where(low, real, imag_t).astype(BF16)
                out_ref[n, at : at + 64, 128:] = jnp.where(low, real_t, imag).astype(BF16)
                out_ref[n, at + 64 : at + 128, :128] = jnp.where(low, -imag, real_t).astype(BF16)
                out_ref[n, at + 64 : at + 128, 128:] = jnp.where(low, -imag_t, real).astype(BF16)


def analyse(number, field, table_ref, factor_of, out_ref, packed):
    for k in SETS[number]:
        first = k // 3
        columns = []
        for lon in range(2):
            pieces = [
                field[(2 * s + lon) * 288 + k * JD : (2 * s + lon) * 288 + k * JD + JD, :]
                for s in range(16)
            ]
            columns.append(jnp.concatenate(pieces, axis=0).astype(BF16))
        data = jnp.concatenate(columns, axis=1)
        rows = table_ref[k * L + 96 * first : (k + 1) * L, :]
        result = jnp.dot(rows, data, preferred_element_type=F32)
        if factor_of is not None:
            result = result * factor_of(k)
        for group in range(first, 4):
            for i in range(3):
                at = ((group - first) * 3 + i) * 32
                for lon in range(2):
                    packed[pl.ds(ROWS[k, group, i, lon], 32, stride=ALL_ROWS), :] = result[
                        at : at + 32, 128 * lon : 128 * lon + 128
                    ]
    narrow(packed, out_ref, ALL_ROWS, SET_ROWS * number, SET_ROWS)


def degree_rows(held, slots, group, i):
    parts = []
    for lon in range(2):
        pieces = [held[pl.ds(ROWS[k, group, i, lon], 32, stride=ALL_ROWS), :] for k in slots]
        parts.append(jnp.concatenate(pieces, axis=0).astype(BF16))
    return jnp.concatenate(parts, axis=1)


def mix(number, grad_ref, matrix_ref, out_ref, held, packed):
    widen(grad_ref, held, ALL_ROWS, SET_ROWS * number, SET_ROWS)
    for group in range(4):
        slots = [k for k in SETS[number] if k // 3 <= group]
        if not slots:
            continue
        for i in range(3):
            mixed = lax.dot_general(
                degree_rows(held, slots, group, i),
                matrix_ref[group * 3 + i],
                (((1,), (1,)), ((), ())),
                preferred_element_type=F32,
            )
            for n, k in enumerate(slots):
                for lon in range(2):
                    packed[pl.ds(ROWS[k, group, i, lon], 32, stride=ALL_ROWS), :] = mixed[
                        32 * n : 32 * n + 32, 128 * lon : 128 * lon + 128
                    ]
    narrow(packed, out_ref, ALL_ROWS, SET_ROWS * number, SET_ROWS)


def weight_grads(held_c, held_g, out_ref):
    low = low_half((64, 128))
    for group in range(4):
        for i in range(3):
            slots = range(3 * group + 3)
            product = lax.dot_general(
                degree_rows(held_c, slots, group, i),
                degree_rows(held_g, slots, group, i),
                (((0,), (0,)), ((), ())),
                preferred_element_type=F32,
            ) * 0.125
            for lon in range(2):
                turned = []
                for half in range(2):
                    lanes = slice(128 * half, 128 * half + 128)
                    with_real = product[128 * lon : 128 * lon + 64, lanes]
                    with_imag = pltpu.roll(product[128 * lon + 64 : 128 * lon + 128, lanes], 64, 1)
                    turned.append(jnp.where(low, with_real + with_imag, with_real - with_imag))
                first, second = turned
                out_ref[2 * group + lon, 128 * i : 128 * i + 64, :] = jnp.where(
                    low, first, pltpu.roll(second, 64, 1)
                ).astype(BF16)
                out_ref[2 * group + lon, 128 * i + 64 : 128 * i + 128, :] = jnp.where(
                    low, pltpu.roll(first, 64, 1), second
                ).astype(BF16)


def synthesise(number, mixed_ref, table_ref, quad_ref, out_ref, held, grid):
    widen(mixed_ref, held, ALL_ROWS, SET_ROWS * number, SET_ROWS)
    for k in SETS[number]:
        first = k // 3
        parts = []
        for lon in range(2):
            pieces = [
                held[pl.ds(ROWS[k, group, i, lon], 32, stride=ALL_ROWS), :]
                for group in range(first, 4)
                for i in range(3)
            ]
            parts.append(jnp.concatenate(pieces, axis=0).astype(BF16))
        data = jnp.concatenate(parts, axis=1)
        rows = table_ref[k * L + 96 * first : (k + 1) * L, :]
        result = lax.dot_general(
            rows, data, (((0,), (0,)), ((), ())), preferred_element_type=F32
        )
        for lon in range(2):
            scaled = result[:, 128 * lon : 128 * lon + 128] * quad_ref[...]
            for s in range(16):
                at = (2 * s + lon) * 288 + k * JD
                grid[at : at + JD, :] = scaled[s * JD : s * JD + JD]
    slots = SETS[number]
    narrow(grid, out_ref, 288, slots[0] * JD, len(slots) * JD)


def inverse(spec_ref, fourier_ref, out_ref, held, turned):
    widen(spec_ref, held, 288, 0, 288)

    def body(step, _):
        for jj in range(4):
            block = held[pl.ds(4 * step + jj, L, stride=JD), :]
            flipped = jnp.transpose(block).astype(BF16)
            turned[64 * jj : 64 * jj + 64, :L] = flipped[:64]
            turned[64 * jj : 64 * jj + 64, L:] = flipped[64:]
        field = jnp.dot(turned[...], fourier_ref[...], preferred_element_type=F32)
        out_ref[pl.ds(4 * step, 4)] = field.astype(BF16).reshape(4, 64, NLON)
        return 0

    lax.fori_loop(0, JD // 4, body, 0)


def kernel(
    inputs_hbm,
    cotangent_hbm,
    weight_hbm,
    fourier_hbm,
    seed_hbm,
    unscale_hbm,
    cos_hbm,
    quad_hbm,
    field_ref,
    weight_grad_ref,
    inputs_ref,
    cotangent_ref,
    weight_ref,
    fourier_ref,
    seed_ref,
    unscale_ref,
    cos_ref,
    quad_ref,
    table_ref,
    gathered,
    matrices,
    near_out,
    near_in,
    field_out,
    field_in,
    grid_in,
    degree_out,
    degree_in,
    partial_out,
    partial_in,
    turned,
    pool,
    loaded,
    order_sent,
    order_got,
    degree_sent,
    degree_got,
    z_sent,
    z_got,
):
    z, y, dp = position()
    lat_rank = (z // 2) * 4 + y
    me_order = lat_rank * 2 + lax.rem(z, 2)
    me_degree = y * 8 + dp
    mesh_ids = pl.DeviceIdType.MESH
    wide = pool.at[pl.ds(0, OWNERS * 288)]
    packed_a = pool.at[pl.ds(OWNERS * 288, OWNERS * ALL_ROWS)]
    packed_b = pool.at[pl.ds(OWNERS * (288 + ALL_ROWS), OWNERS * ALL_ROWS)]
    order_rows = [(slots[0] * JD, len(slots) * JD) for slots in SETS]

    loads = [
        (cotangent_hbm, cotangent_ref),
        (fourier_hbm, fourier_ref),
        (weight_hbm, weight_ref),
        (inputs_hbm, inputs_ref),
        (seed_hbm.at[me_order], seed_ref),
        (unscale_hbm.at[me_order], unscale_ref),
        (cos_hbm, cos_ref),
        (quad_hbm, quad_ref),
    ]
    loads = [pltpu.make_async_copy(a, b, loaded.at[n]) for n, (a, b) in enumerate(loads)]

    def order_peer(t):
        at = lax.rem(t * 13, 32)
        return lax.rem(z + lax.rem(at, 8), 8), lax.rem(y + at // 8, 4)

    def degree_peer(t):
        at = lax.rem(t * 13, 32)
        return lax.rem(y + lax.rem(at, 4), 4), lax.rem(dp + at // 4, 8)

    def order_copy(n, src, dst, t, first=0, rows=288):
        pz, py = order_peer(t)
        return pltpu.make_async_remote_copy(
            src_ref=src.at[((pz // 2) * 4 + py) * 2 + lax.rem(pz, 2), pl.ds(first, rows)],
            dst_ref=dst.at[me_order, pl.ds(first, rows)],
            send_sem=order_sent.at[n, t],
            recv_sem=order_got.at[n, t],
            device_id=place(pz, py, dp),
            device_id_type=mesh_ids,
        )

    def cotangent_copy(t):
        return order_copy(0, near_out, near_in, t)

    def field_copy(t):
        return order_copy(1, field_out, field_in, t)

    def grid_copy(number, t):
        return order_copy(2 + number, near_out, grid_in, t, *order_rows[number])

    def degree_copy(n, number, t):
        py, pd = degree_peer(t)
        return pltpu.make_async_remote_copy(
            src_ref=degree_out.at[n, py * 8 + pd, pl.ds(SET_ROWS * number, SET_ROWS)],
            dst_ref=degree_in.at[n, me_degree, pl.ds(SET_ROWS * number, SET_ROWS)],
            send_sem=degree_sent.at[2 * n + number, t],
            recv_sem=degree_got.at[2 * n + number, t],
            device_id=place(z, py, pd),
            device_id_type=mesh_ids,
        )

    def weight_copy(t):
        return pltpu.make_async_remote_copy(
            src_ref=weight_ref,
            dst_ref=gathered.at[z],
            send_sem=z_sent.at[0, t],
            recv_sem=z_got.at[0, t],
            device_id=place(lax.rem(z + t, 8), y, dp),
            device_id_type=mesh_ids,
        )

    def partial_copy(t):
        pz = lax.rem(z + t, 8)
        return pltpu.make_async_remote_copy(
            src_ref=partial_out.at[pz],
            dst_ref=partial_in.at[z],
            send_sem=z_sent.at[1, t],
            recv_sem=z_got.at[1, t],
            device_id=place(pz, y, dp),
            device_id_type=mesh_ids,
        )

    def each(first, end, action):
        def body(t, _):
            action(t)
            return 0

        lax.fori_loop(first, end, body, 0)

    def send_field(first, end):
        each(first, end, lambda t: field_copy(t).start())

    def send_grid(number, first, end):
        each(first, end, lambda t: grid_copy(number, t).start())

    def send_degrees(n, number):
        each(1, 32, lambda t: degree_copy(n, number, t).start())
        rows = slice(SET_ROWS * number, SET_ROWS * number + SET_ROWS)
        degree_in[n, me_degree, rows, :] = degree_out[n, me_degree, rows, :]

    def wait_degrees(n, number):
        each(1, 32, lambda t: degree_copy(n, number, t).wait())

    def keep_grid(number):
        first, rows = order_rows[number]
        grid_in[me_order, first : first + rows, :] = near_out[me_order, first : first + rows, :]

    def factor_of(k):
        base = 1.0 / math.sqrt(NLAT)
        return jnp.where(me_order == 0, base, 2.0 * base) if k == 0 else 2.0 * base

    for load in loads:
        load.start()
    barrier = pltpu.get_barrier_semaphore()

    def greet(t):
        pz, py = order_peer(t)
        pl.semaphore_signal(barrier, inc=1, device_id=place(pz, py, dp), device_id_type=mesh_ids)
        py, pd = degree_peer(t)
        pl.semaphore_signal(barrier, inc=1, device_id=place(z, py, pd), device_id_type=mesh_ids)

    each(1, 32, greet)
    loads[2].wait()
    pl.semaphore_wait(barrier, 62)
    each(1, 8, lambda t: weight_copy(t).start())
    gathered[z] = weight_ref[...]
    loads[0].wait()
    loads[1].wait()

    transform(cotangent_ref, fourier_ref, near_out, wide, None)
    each(1, 32, lambda t: cotangent_copy(t).start())
    near_in[me_order] = near_out[me_order]
    for load in loads[3:]:
        load.wait()
    legendre(me_order, seed_ref, unscale_ref, cos_ref, table_ref, pool)
    transform(
        inputs_ref,
        fourier_ref,
        field_out,
        wide,
        lambda j: quad_ref[pl.ds(lat_rank * JD + j, 1), :],
    )
    field_in[me_order] = field_out[me_order]
    each(1, 8, lambda t: weight_copy(t).wait())
    mixing_matrices(gathered, matrices)
    packed_a[...] = jnp.zeros((OWNERS * ALL_ROWS, 128), F32)
    packed_b[...] = jnp.zeros((OWNERS * ALL_ROWS, 128), F32)
    each(1, 32, lambda t: cotangent_copy(t).wait())

    send_field(1, 7)
    widen(near_in, wide, 288, 0, 288)
    analyse(0, wide, table_ref, factor_of, degree_out.at[0], packed_a)
    send_degrees(0, 0)
    send_field(7, 11)
    analyse(1, wide, table_ref, factor_of, degree_out.at[0], packed_a)
    send_degrees(0, 1)
    send_field(11, 17)
    wait_degrees(0, 0)
    mix(0, degree_in.at[0], matrices, degree_out.at[1], packed_b, packed_a)
    send_degrees(1, 0)
    send_field(17, 24)
    wait_degrees(0, 1)
    mix(1, degree_in.at[0], matrices, degree_out.at[1], packed_b, packed_a)
    send_degrees(1, 1)
    send_field(24, 32)
    wait_degrees(1, 0)
    synthesise(0, degree_in.at[1], table_ref, quad_ref, near_out, packed_b, wide)
    send_grid(0, 1, 32)
    keep_grid(0)
    wait_degrees(1, 1)
    synthesise(1, degree_in.at[1], table_ref, quad_ref, near_out, packed_b, wide)
    send_grid(1, 1, 9)
    keep_grid(1)

    each(1, 32, lambda t: field_copy(t).wait())
    widen(field_in, wide, 288, 0, 288)
    analyse(0, wide, table_ref, None, degree_out.at[2], packed_a)
    send_degrees(2, 0)
    analyse(1, wide, table_ref, None, degree_out.at[2], packed_a)
    send_degrees(2, 1)
    send_grid(1, 9, 32)
    widen(degree_in.at[0], packed_b, ALL_ROWS, 0, ALL_ROWS)
    wait_degrees(2, 0)
    wait_degrees(2, 1)
    widen(degree_in.at[2], packed_a, ALL_ROWS, 0, ALL_ROWS)
    weight_grads(packed_a, packed_b, partial_out)
    each(1, 8, lambda t: partial_copy(t).start())
    partial_in[z] = partial_out[z]
    each(1, 32, lambda t: grid_copy(0, t).wait())
    each(1, 32, lambda t: grid_copy(1, t).wait())
    inverse(grid_in, fourier_ref, field_ref, wide, turned)
    each(1, 8, lambda t: partial_copy(t).wait())
    total = partial_in[0].astype(F32)
    for n in range(1, 8):
        total = total + partial_in[n].astype(F32)
    weight_grad_ref[...] = total


def shards(inputs, cotangent, weight):
    seed, unscale = legendre_seeds()
    lat = np.arange(NLAT, dtype=np.float64)
    angle = math.pi * (lat + 0.5) / NLAT
    quad = (2.0 * math.pi * np.sin(angle) / math.sqrt(NLAT)).astype(np.float32)
    quad = np.broadcast_to(quad[:, None], (NLAT, 128))
    cosine = np.broadcast_to(np.cos(angle).astype(np.float32)[None, :], (16, NLAT))
    vmem = pl.BlockSpec(memory_space=pltpu.VMEM)
    anywhere = pl.BlockSpec(memory_space=pl.ANY)
    chunks = pltpu.VMEM((OWNERS, 288, 128), BF16)
    degrees = pltpu.VMEM((3, OWNERS, ALL_ROWS, 128), BF16)
    dma = pltpu.SemaphoreType.DMA
    field, weight_grad = pl.pallas_call(
        kernel,
        in_specs=[anywhere] * 8,
        out_specs=[vmem, vmem],
        out_shape=[
            jax.ShapeDtypeStruct((JD, 64, NLON), BF16),
            jax.ShapeDtypeStruct((L, 128), F32),
        ],
        scratch_shapes=[
            pltpu.VMEM((JD, 64, NLON), BF16),
            pltpu.VMEM((JD, 64, NLON), BF16),
            pltpu.VMEM((L, 128), BF16),
            pltpu.VMEM((2 * L, NLON), BF16),
            pltpu.VMEM((16, NLAT), F32),
            pltpu.VMEM((16, NLAT), F32),
            pltpu.VMEM((16, NLAT), F32),
            pltpu.VMEM((NLAT, 128), F32),
            pltpu.VMEM((SLOTS * L, NLAT), BF16),
            pltpu.VMEM((8, L, 128), BF16),
            pltpu.VMEM((12, 256, 256), BF16),
            chunks,
            chunks,
            chunks,
            chunks,
            chunks,
            degrees,
            degrees,
            pltpu.VMEM((8, L, 128), BF16),
            pltpu.VMEM((8, L, 128), BF16),
            pltpu.VMEM((256, 2 * L), BF16),
            pltpu.VMEM((OWNERS * (288 + 2 * ALL_ROWS), 128), F32),
            dma((8,)),
            dma((4, 32)),
            dma((4, 32)),
            dma((6, 32)),
            dma((6, 32)),
            dma((2, 8)),
            dma((2, 8)),
        ],
        compiler_params=pltpu.CompilerParams(
            vmem_limit_bytes=60 * MIB, collective_id=1, has_side_effects=True
        ),
        cost_estimate=pl.CostEstimate(
            flops=13_000_000_000, bytes_accessed=16_000_000, transcendentals=0
        ),
        name="sphere",
    )(
        inputs[0],
        cotangent[0],
        weight.reshape(L, 128),
        jnp.asarray(fourier_rows()),
        jnp.asarray(seed),
        jnp.asarray(unscale),
        jnp.asarray(cosine),
        jnp.asarray(quad),
    )
    return field[None], weight_grad.reshape(3, 2, 64, 128)


def solution(mesh):
    fine = Mesh(mesh.devices.reshape(4, 4, 2, 8), ("zh", "y", "lon", "dp"))
    field = P("dp", ("zh", "y"), "lon", None)
    spectral = P(("zh", "y", "dp"), None, "lon", None)
    return jax.shard_map(
        shards,
        mesh=fine,
        in_specs=(field, field, spectral),
        out_specs=(field, spectral),
        check_vma=False,
    )
```

time: 378 us -> 231 us (0.61)
  Pallas kernels: 66.1 us -> 219 us
  waiting for transfers between devices: 133 us -> 0 us
  blocking collectives: 76.1 us -> 0 us
  starting transfers between devices: 49.5 us -> 0 us
  local copies, waits for them, and re-layouts: 33.3 us -> 6.79 us
  between operations: 14.4 us -> 0.65 us
    pallas_call x9 -> x1, Pallas kernels: 66.1 us -> 219 us  [shards(): pl.pallas_call(kernel, in_specs=[anywhere] * 8, out_specs=[vmem, vmem], o...]
    all_to_all x6 -> x0, waiting for transfers between devices: 133 us -> none  [exchange(): return lax.all_to_all(x, axes, split_axis=0, concat_axis=0, tiled=True)]
    all_gather x1 -> x0, blocking collectives: 76.1 us -> none  [shards(): gathered = lax.all_gather(weight, ('zh', 'lon'), axis=0, tiled=False)]
    all_to_all x6 -> x0, starting transfers between devices: 49.5 us -> none  [exchange(): return lax.all_to_all(x, axes, split_axis=0, concat_axis=0, tiled=True)]
    unnamed x30 -> x4, local copies, waits for them, and re-layouts: 13.7 us -> 4.02 us
    reshape x3 -> x0, local copies, waits for them, and re-layouts: 9.33 us -> none  [the longest x1 6.04 us: mixing_matrices(): return both.transpose(0, 2, 1, 3, 4, 5, 6, 7).reshape(12, 256, 256)]
    transpose x1 -> x0, local copies, waits for them, and re-layouts: 4.91 us -> none  [mixing_matrices(): return both.transpose(0, 2, 1, 3, 4, 5, 6, 7).reshape(12, 256, 256)]
  transfers between devices with their start and end apart: 7 -> 0, of which waited for: 5 -> 0; matrix products, arithmetic and copies ran while one was open for 6% -> 0% of each run, Pallas kernels for 14% -> 0%
where the time goes in v3:
time: 231 us; the launch traced here: 227 us
  Pallas kernels  219 us (95%)
  local copies, waits for them, and re-layouts  6.79 us (3%)
    pallas_call x1, Pallas kernels, shards(): pl.pallas_call(kernel, in_specs=[anywhere] * 8, out_specs=[vmem, vmem], o...  219 us

profile of v3, /device:TPU:18, one launch (start us, length us, event | category | flops | bytes accessed | tf_op | source)
XLA Modules:
  0.0 226.7 jit_solution(14391461616325154352)
XLA Ops:
  0.6 1.3 jit_solution_.6.cos_hbm
  1.9 1.5 jit_solution_.7.quad_hbm
  3.4 219.2 %sphere.1 = (bf16[24,64,768]{2,1,0:T(8,128)(2,1)}, f32[384,128]{1,0:T(8,128)}) custom-call(bf16[24,64,768]{2,1,0:T(8,128)(2,1)} %bitcast.7, bf16[24,64,768]{2,1,0:T(8,128)(2,1)} %bitcast.8, bf16[384,128]{1,0:T(8,128)(2,1)} %bitcast.9, bf16[768,768]{1,0:T(8,128)(2,1)} %constant.10.clone.fourier_hbm, f32[32,16,384]{2,1,0:T(8,128)} %constant.11.clone.seed_hbm, ...), custom_call_target="tpu_custom_call" | custom-call | flops 12999999488 | bytes 16000000 | tf_op jit(solution)/shard_map/sphere/pallas_call | solution.py:570
  222.6 0.0 copy-start
  222.7 3.3 %copy.12 = bf16[1,24,64,768]{3,2,1,0:T(8,128)(2,1)} copy(bf16[1,24,64,768]{3,2,1,0:T(8,128)(2,1)} %bitcast.5) | data formatting | bytes 4718592
  226.0 0.0 copy-done
  226.0 0.7 copy.13
Async XLA Ops:
  222.6 3.4 %copy-start = (f32[384,128]{1,0:T(8,128)S(1)}, f32[384,128]{1,0:T(8,128)}, u32[]{:S(2)}) copy-start(f32[384,128]{1,0:T(8,128)} %get-tuple-element.5) | copy-start | bytes 589828

commit v4 on v3

--- a/solution.py
+++ b/solution.py
@@ -28,6 +28,8 @@
 
 SETS = (range(0, 4), range(4, SLOTS))
 SET_ROWS = 96
+FIELD_SENT = (31, 31, 31, 31, 31)
+GRID_SENT = (8, 8, 31)
 HALF_ROWS = 48
 ALL_ROWS = 192
 
@@ -70,7 +72,7 @@
     shift = np.clip(-log_start - 60.0, 0.0, 80.0)
     seed = np.exp(log_start + shift)
     seed = np.where(seed < 1.2e-38, 0.0, seed)
-    return seed.astype(np.float32), np.exp(-shift).astype(np.float32)
+    return np.concatenate([seed, np.exp(-shift)], axis=1).astype(np.float32).reshape(-1, NLAT)
 
 
 def low_half(shape):
@@ -104,7 +106,7 @@
     lax.fori_loop(0, OWNERS, body, 0)
 
 
-def transform(x_ref, fourier_ref, out_ref, held, scale_of):
+def transform(x_ref, fourier_ref, held, scale_of, first, end):
     low = low_half((L, 128))
 
     def body(step, _):
@@ -122,8 +124,7 @@
         held[pl.ds(2 * step + 1, L, stride=JD), :] = odd
         return 0
 
-    lax.fori_loop(0, JD // 2, body, 0)
-    narrow(held, out_ref, 288, 0, 288)
+    lax.fori_loop(first, end, body, 0)
 
 
 def legendre(owner, seed_ref, unscale_ref, cos_ref, out_ref, pool):
@@ -321,10 +322,7 @@
     cotangent_hbm,
     weight_hbm,
     fourier_hbm,
-    seed_hbm,
-    unscale_hbm,
-    cos_hbm,
-    quad_hbm,
+    constants_hbm,
     field_ref,
     weight_grad_ref,
     inputs_ref,
@@ -334,6 +332,7 @@
     seed_ref,
     unscale_ref,
     cos_ref,
+    quad_wide,
     quad_ref,
     table_ref,
     gathered,
@@ -372,10 +371,10 @@
         (fourier_hbm, fourier_ref),
         (weight_hbm, weight_ref),
         (inputs_hbm, inputs_ref),
-        (seed_hbm.at[me_order], seed_ref),
-        (unscale_hbm.at[me_order], unscale_ref),
-        (cos_hbm, cos_ref),
-        (quad_hbm, quad_ref),
+        (constants_hbm.at[pl.ds(pl.multiple_of(me_order * 32, 32), 16)], seed_ref),
+        (constants_hbm.at[pl.ds(pl.multiple_of(me_order * 32 + 16, 16), 16)], unscale_ref),
+        (constants_hbm.at[pl.ds(OWNERS * 32, 16)], cos_ref),
+        (constants_hbm.at[pl.ds(OWNERS * 32 + 16, 128)], quad_wide),
     ]
     loads = [pltpu.make_async_copy(a, b, loaded.at[n]) for n, (a, b) in enumerate(loads)]
 
@@ -418,15 +417,30 @@
             device_id_type=mesh_ids,
         )
 
-    def weight_copy(t):
-        return pltpu.make_async_remote_copy(
-            src_ref=weight_ref,
-            dst_ref=gathered.at[z],
-            send_sem=z_sent.at[0, t],
-            recv_sem=z_got.at[0, t],
-            device_id=place(lax.rem(z + t, 8), y, dp),
-            device_id_type=mesh_ids,
-        )
+    def weight_copies(step):
+        copies = []
+        for sign, last, base in ((1, 4, 0), (-1, 3, 4)):
+            if step > last:
+                continue
+            block = lax.rem(z + 8 - sign * (step - 1), 8)
+            copies.append(
+                pltpu.make_async_remote_copy(
+                    src_ref=gathered.at[block],
+                    dst_ref=gathered.at[block],
+                    send_sem=z_sent.at[0, base + step],
+                    recv_sem=z_got.at[0, base + step],
+                    device_id=place(lax.rem(z + 8 + sign, 8), y, dp),
+                    device_id_type=mesh_ids,
+                )
+            )
+        return copies
+
+    def forward_weights(step):
+        if step > 1:
+            for copy in weight_copies(step - 1):
+                copy.wait_recv()
+        for copy in weight_copies(step):
+            copy.start()
 
     def partial_copy(t):
         pz = lax.rem(z + t, 8)
@@ -447,10 +461,10 @@
         lax.fori_loop(first, end, body, 0)
 
     def send_field(first, end):
-        each(first, end, lambda t: field_copy(t).start())
+        each(first + 1, end + 1, lambda t: field_copy(t).start())
 
     def send_grid(number, first, end):
-        each(first, end, lambda t: grid_copy(number, t).start())
+        each(first + 1, end + 1, lambda t: grid_copy(number, t).start())
 
     def send_degrees(n, number):
         each(1, 32, lambda t: degree_copy(n, number, t).start())
@@ -481,66 +495,83 @@
     each(1, 32, greet)
     loads[2].wait()
     pl.semaphore_wait(barrier, 62)
-    each(1, 8, lambda t: weight_copy(t).start())
     gathered[z] = weight_ref[...]
+    forward_weights(1)
     loads[0].wait()
     loads[1].wait()
 
-    transform(cotangent_ref, fourier_ref, near_out, wide, None)
+    transform(cotangent_ref, fourier_ref, wide, None, 0, 5)
+    forward_weights(2)
+    transform(cotangent_ref, fourier_ref, wide, None, 5, 9)
+    forward_weights(3)
+    transform(cotangent_ref, fourier_ref, wide, None, 9, JD // 2)
+    narrow(wide, near_out, 288, 0, 288)
+    forward_weights(4)
     each(1, 32, lambda t: cotangent_copy(t).start())
     near_in[me_order] = near_out[me_order]
     for load in loads[3:]:
         load.wait()
+    for c in range(3):
+        quad_ref[128 * c : 128 * c + 128, :] = quad_wide[:, 128 * c : 128 * c + 128]
     legendre(me_order, seed_ref, unscale_ref, cos_ref, table_ref, pool)
     transform(
         inputs_ref,
         fourier_ref,
-        field_out,
         wide,
         lambda j: quad_ref[pl.ds(lat_rank * JD + j, 1), :],
+        0,
+        JD // 2,
     )
+    narrow(wide, field_out, 288, 0, 288)
     field_in[me_order] = field_out[me_order]
-    each(1, 8, lambda t: weight_copy(t).wait())
+    send_field(0, FIELD_SENT[0])
+    for step in range(1, 5):
+        for copy in weight_copies(step):
+            copy.wait_send()
+    for copy in weight_copies(4):
+        copy.wait_recv()
     mixing_matrices(gathered, matrices)
     packed_a[...] = jnp.zeros((OWNERS * ALL_ROWS, 128), F32)
     packed_b[...] = jnp.zeros((OWNERS * ALL_ROWS, 128), F32)
     each(1, 32, lambda t: cotangent_copy(t).wait())
 
-    send_field(1, 7)
     widen(near_in, wide, 288, 0, 288)
     analyse(0, wide, table_ref, factor_of, degree_out.at[0], packed_a)
     send_degrees(0, 0)
-    send_field(7, 11)
+    send_field(FIELD_SENT[0], FIELD_SENT[1])
     analyse(1, wide, table_ref, factor_of, degree_out.at[0], packed_a)
     send_degrees(0, 1)
-    send_field(11, 17)
+    send_field(FIELD_SENT[1], FIELD_SENT[2])
     wait_degrees(0, 0)
     mix(0, degree_in.at[0], matrices, degree_out.at[1], packed_b, packed_a)
     send_degrees(1, 0)
-    send_field(17, 24)
+    send_field(FIELD_SENT[2], FIELD_SENT[3])
     wait_degrees(0, 1)
     mix(1, degree_in.at[0], matrices, degree_out.at[1], packed_b, packed_a)
     send_degrees(1, 1)
-    send_field(24, 32)
+    send_field(FIELD_SENT[3], FIELD_SENT[4])
     wait_degrees(1, 0)
     synthesise(0, degree_in.at[1], table_ref, quad_ref, near_out, packed_b, wide)
-    send_grid(0, 1, 32)
+    send_field(FIELD_SENT[4], 31)
+    send_grid(0, 0, 31)
     keep_grid(0)
     wait_degrees(1, 1)
     synthesise(1, degree_in.at[1], table_ref, quad_ref, near_out, packed_b, wide)
-    send_grid(1, 1, 9)
+    send_grid(1, 0, GRID_SENT[0])
     keep_grid(1)
 
     each(1, 32, lambda t: field_copy(t).wait())
     widen(field_in, wide, 288, 0, 288)
     analyse(0, wide, table_ref, None, degree_out.at[2], packed_a)
     send_degrees(2, 0)
+    send_grid(1, GRID_SENT[0], GRID_SENT[1])
     analyse(1, wide, table_ref, None, degree_out.at[2], packed_a)
     send_degrees(2, 1)
-    send_grid(1, 9, 32)
+    send_grid(1, GRID_SENT[1], GRID_SENT[2])
     widen(degree_in.at[0], packed_b, ALL_ROWS, 0, ALL_ROWS)
     wait_degrees(2, 0)
     wait_degrees(2, 1)
+    send_grid(1, GRID_SENT[2], 31)
     widen(degree_in.at[2], packed_a, ALL_ROWS, 0, ALL_ROWS)
     weight_grads(packed_a, packed_b, partial_out)
     each(1, 8, lambda t: partial_copy(t).start())
@@ -556,12 +587,12 @@
 
 
 def shards(inputs, cotangent, weight):
-    seed, unscale = legendre_seeds()
     lat = np.arange(NLAT, dtype=np.float64)
     angle = math.pi * (lat + 0.5) / NLAT
     quad = (2.0 * math.pi * np.sin(angle) / math.sqrt(NLAT)).astype(np.float32)
-    quad = np.broadcast_to(quad[:, None], (NLAT, 128))
+    quad = np.repeat(quad.reshape(3, 128).T, 128, axis=1)
     cosine = np.broadcast_to(np.cos(angle).astype(np.float32)[None, :], (16, NLAT))
+    constants = np.concatenate([legendre_seeds(), cosine, quad], axis=0)
     vmem = pl.BlockSpec(memory_space=pltpu.VMEM)
     anywhere = pl.BlockSpec(memory_space=pl.ANY)
     chunks = pltpu.VMEM((OWNERS, 288, 128), BF16)
@@ -569,7 +600,7 @@
     dma = pltpu.SemaphoreType.DMA
     field, weight_grad = pl.pallas_call(
         kernel,
-        in_specs=[anywhere] * 8,
+        in_specs=[anywhere] * 5,
         out_specs=[vmem, vmem],
         out_shape=[
             jax.ShapeDtypeStruct((JD, 64, NLON), BF16),
@@ -583,6 +614,7 @@
             pltpu.VMEM((16, NLAT), F32),
             pltpu.VMEM((16, NLAT), F32),
             pltpu.VMEM((16, NLAT), F32),
+            pltpu.VMEM((128, NLAT), F32),
             pltpu.VMEM((NLAT, 128), F32),
             pltpu.VMEM((SLOTS * L, NLAT), BF16),
             pltpu.VMEM((8, L, 128), BF16),
@@ -618,10 +650,7 @@
         cotangent[0],
         weight.reshape(L, 128),
         jnp.asarray(fourier_rows()),
-        jnp.asarray(seed),
-        jnp.asarray(unscale),
-        jnp.asarray(cosine),
-        jnp.asarray(quad),
+        jnp.asarray(constants),
     )
     return field[None], weight_grad.reshape(3, 2, 64, 128)
 

time: 231 us -> 222 us (0.961)
  Pallas kernels: 219 us -> 213 us
  local copies, waits for them, and re-layouts: 6.79 us -> 4.02 us
    pallas_call x1, Pallas kernels: 219 us -> 213 us  [shards(): pl.pallas_call(kernel, in_specs=[anywhere] * 5, out_specs=[vmem, vmem], o...]
    another operation x2 -> x0, local copies, waits for them, and re-layouts: 2.77 us -> none
where the time goes in v4:
time: 222 us; the launch traced here: 217 us
  Pallas kernels  213 us (96%)
  local copies, waits for them, and re-layouts  4.02 us (2%)
    pallas_call x1, Pallas kernels, shards(): pl.pallas_call(kernel, in_specs=[anywhere] * 5, out_specs=[vmem, vmem], o...  213 us

profile of v4, /device:TPU:18, one launch (start us, length us, event | category | flops | bytes accessed | tf_op | source)
XLA Modules:
  0.0 217.4 jit_solution(12382294334753003600)
XLA Ops:
  0.6 212.8 %sphere.1 = (bf16[24,64,768]{2,1,0:T(8,128)(2,1)}, f32[384,128]{1,0:T(8,128)}) custom-call(bf16[24,64,768]{2,1,0:T(8,128)(2,1)} %bitcast.7, bf16[24,64,768]{2,1,0:T(8,128)(2,1)} %bitcast.8, bf16[384,128]{1,0:T(8,128)(2,1)} %bitcast.9, bf16[768,768]{1,0:T(8,128)(2,1)} %constant.4.clone.fourier_hbm, f32[1168,384]{1,0:T(8,128)} %constant.5.clone.constants_hbm), custom_call_target="tpu_custom_call" | custom-call | flops 12999999488 | bytes 16000000 | tf_op jit(solution)/shard_map/sphere/pallas_call | solution.py:601
  213.4 0.0 copy-start
  213.4 3.3 %copy.9 = bf16[1,24,64,768]{3,2,1,0:T(8,128)(2,1)} copy(bf16[1,24,64,768]{3,2,1,0:T(8,128)(2,1)} %bitcast.5) | data formatting | bytes 4718592
  216.8 0.0 copy-done
  216.8 0.7 copy.10
Async XLA Ops:
  213.4 3.4 %copy-start = (f32[384,128]{1,0:T(8,128)S(1)}, f32[384,128]{1,0:T(8,128)}, u32[]{:S(2)}) copy-start(f32[384,128]{1,0:T(8,128)} %get-tuple-element.5) | copy-start | bytes 589828

commit v5 on v4

--- a/solution.py
+++ b/solution.py
@@ -28,7 +28,7 @@
 
 SETS = (range(0, 4), range(4, SLOTS))
 SET_ROWS = 96
-FIELD_SENT = (31, 31, 31, 31, 31)
+FIELD_SENT = (8, 16, 24, 31, 31)
 GRID_SENT = (8, 8, 31)
 HALF_ROWS = 48
 ALL_ROWS = 192
@@ -323,8 +323,9 @@
     weight_hbm,
     fourier_hbm,
     constants_hbm,
+    field_hbm,
+    weight_grad_ref,
     field_ref,
-    weight_grad_ref,
     inputs_ref,
     cotangent_ref,
     weight_ref,
@@ -579,11 +580,14 @@
     each(1, 32, lambda t: grid_copy(0, t).wait())
     each(1, 32, lambda t: grid_copy(1, t).wait())
     inverse(grid_in, fourier_ref, field_ref, wide, turned)
+    store = pltpu.make_async_copy(field_ref, field_hbm, loaded.at[0])
+    store.start()
     each(1, 8, lambda t: partial_copy(t).wait())
     total = partial_in[0].astype(F32)
     for n in range(1, 8):
         total = total + partial_in[n].astype(F32)
     weight_grad_ref[...] = total
+    store.wait()
 
 
 def shards(inputs, cotangent, weight):
@@ -601,12 +605,13 @@
     field, weight_grad = pl.pallas_call(
         kernel,
         in_specs=[anywhere] * 5,
-        out_specs=[vmem, vmem],
+        out_specs=[anywhere, vmem],
         out_shape=[
             jax.ShapeDtypeStruct((JD, 64, NLON), BF16),
             jax.ShapeDtypeStruct((L, 128), F32),
         ],
         scratch_shapes=[
+            pltpu.VMEM((JD, 64, NLON), BF16),
             pltpu.VMEM((JD, 64, NLON), BF16),
             pltpu.VMEM((JD, 64, NLON), BF16),
             pltpu.VMEM((L, 128), BF16),

time: 222 us -> 219 us (0.986); the launches traced: 217 us -> 220 us
    pallas_call x1, Pallas kernels: 213 us -> 215 us  [shards(): pl.pallas_call(kernel, in_specs=[anywhere] * 5, out_specs=[anywhere, vmem...]
where the time goes in v5:
time: 219 us; the launch traced here: 220 us
  Pallas kernels  215 us (98%)
  local copies, waits for them, and re-layouts  4.02 us (2%)
    pallas_call x1, Pallas kernels, shards(): pl.pallas_call(kernel, in_specs=[anywhere] * 5, out_specs=[anywhere, vmem...  215 us

profile of v5, /device:TPU:18, one launch (start us, length us, event | category | flops | bytes accessed | tf_op | source)
XLA Modules:
  0.0 219.7 jit_solution(11408311313870012011)
XLA Ops:
  0.6 215.0 %sphere.1 = (bf16[24,64,768]{2,1,0:T(8,128)(2,1)}, f32[384,128]{1,0:T(8,128)}) custom-call(bf16[24,64,768]{2,1,0:T(8,128)(2,1)} %bitcast.7, bf16[24,64,768]{2,1,0:T(8,128)(2,1)} %bitcast.8, bf16[384,128]{1,0:T(8,128)(2,1)} %bitcast.9, bf16[768,768]{1,0:T(8,128)(2,1)} %constant.4.clone.fourier_hbm, f32[1168,384]{1,0:T(8,128)} %constant.5.clone.constants_hbm), custom_call_target="tpu_custom_call" | custom-call | flops 12999999488 | bytes 16000000 | tf_op jit(solution)/shard_map/sphere/pallas_call | solution.py:605
  215.7 0.0 copy-start
  215.7 3.3 %copy.9 = bf16[1,24,64,768]{3,2,1,0:T(8,128)(2,1)} copy(bf16[1,24,64,768]{3,2,1,0:T(8,128)(2,1)} %bitcast.5) | data formatting | bytes 4718592
  219.0 0.0 copy-done
  219.0 0.7 copy.10
Async XLA Ops:
  215.7 3.4 %copy-start = (f32[384,128]{1,0:T(8,128)S(1)}, f32[384,128]{1,0:T(8,128)}, u32[]{:S(2)}) copy-start(f32[384,128]{1,0:T(8,128)} %get-tuple-element.5) | copy-start | bytes 589828
